TPU v7x, 256 devices: a whole 4x4x8 slice. The times are simulated.
256 devices in a mesh: lat: 8 (over x, core), lon: 32 (over z, y).
Axes of the slice: x: 4, y: 4, z: 8, core: 2. Of those that a mesh axis runs over, the one named last changes fastest.
Arguments:
- ensemble: float32 [96, 1536, 4, 128], P('lat', 'lon'), may hold values from -6 to 6
- grad_increment: float32 [96, 1536, 128], P('lat', 'lon'), may hold values from -6 to 6
- normalization: float32 [96, 1536], P('lat', 'lon'), may hold values from 12 to 48
- lon_diffusion: float32 [96, 1536], P('lat', 'lon'), may hold values from 1152 to 4608
- lat_diffusion: float32 [96, 1536], P('lat', 'lon'), may hold values from 288 to 1152
- vert_diag: float32 [128], replicated, may hold values from 1 to 2
- vert_sub: float32 [127], replicated, may hold values from -0.8 to -0.3
Outputs:
- grad_alpha: float32 [96, 1536, 4, 128], P('lat', 'lon')
All inputs are finite; a program needn't handle non-finite values.
Results may differ from a plain program's by a relative error of at most 0.0003.
Values sent between devices are 32-bit elements; how exact they have to be, the bound alone decides.
A program may use at most 64 MiB of HBM per device.

v0:
```python
import jax
import jax.numpy as jnp
from jax import lax
from jax.sharding import PartitionSpec as P

HIGHEST = lax.Precision.HIGHEST


def shifted(value, axis, steps):
    count = lax.axis_size(axis)
    pairs = [(source, (source + steps) % count) for source in range(count)]
    return lax.ppermute(value, axis, pairs)


def laid_out(tiles, dim):
    tiles = jnp.moveaxis(tiles, 0, dim)
    dims = tiles.shape
    return tiles.reshape(*dims[:dim], dims[dim] * dims[dim + 1], *dims[dim + 2 :])


def sent_to_all(value, axis):
    copies = jnp.broadcast_to(value, (lax.axis_size(axis), *value.shape))
    return lax.all_to_all(copies, axis, split_axis=0, concat_axis=0, tiled=True)


def collect(value, axis, dim):
    return laid_out(sent_to_all(value, axis), dim)


def shifted_2(value, axis, steps):
    count = lax.axis_size(axis)
    initial, last = (max(0, -steps), min(count, count - steps))
    return lax.ppermute(value, axis, [(source, source + steps) for source in range(initial, last)])


def block_inverse(edges, base_vals):
    block_len = edges.shape[-1]
    row_ids = lax.broadcasted_iota(jnp.int32, (block_len, block_len), 0)
    col_ids = lax.broadcasted_iota(jnp.int32, (block_len, block_len), 1)
    leading = jnp.arange(block_len) == 0
    earlier = jnp.concatenate([jnp.zeros_like(edges[:, :1]), edges[:, :-1]], axis=1)
    diagonal = jnp.where(leading[None, :], 1.0, base_vals + earlier + edges)
    couple_vals = jnp.where(leading[None, :], 0.0, -edges)
    upper_mask = (col_ids == row_ids + 1).astype(jnp.float32)
    eye_mask = (col_ids == row_ids).astype(jnp.float32)
    matrix = (
        diagonal[:, :, None] * eye_mask
        + couple_vals[:, :, None] * upper_mask
        + couple_vals[:, None, :] * upper_mask.T
    )
    factor = jnp.linalg.cholesky(matrix)
    identity = jnp.broadcast_to(eye_mask, matrix.shape)
    inverse = jax.scipy.linalg.cho_solve((factor, True), identity)
    corner = ((row_ids == 0) & (col_ids == 0)).astype(jnp.float32)
    return inverse - corner


def interface_values(inverse, edges, base_vals, first_row, last_row, sep_rhs):
    block_len = inverse.shape[-1]
    left_edge = edges[:, 0]
    right_edge = edges[:, block_len - 1]
    own_diag = base_vals[:, 0] + left_edge - left_edge * left_edge * inverse[:, 1, 1]
    next_diag = right_edge - right_edge * right_edge * inverse[:, block_len - 1, block_len - 1]
    coupling = -left_edge * right_edge * inverse[:, 1, block_len - 1]
    own_rhs = sep_rhs + left_edge[:, None] * first_row
    next_rhs = right_edge[:, None] * last_row
    return (own_diag, next_diag, coupling, own_rhs, next_rhs)


def interface_solve(diag_sum, coupling, rhs_sum):
    part_count = diag_sum.shape[0]
    row_ids = lax.broadcasted_iota(jnp.int32, (part_count, part_count), 0)
    col_ids = lax.broadcasted_iota(jnp.int32, (part_count, part_count), 1)
    follow = (col_ids == (row_ids + 1) % part_count).astype(jnp.float32)
    eye_mask = (col_ids == row_ids).astype(jnp.float32)
    diag_t = diag_sum.T
    couple_t = coupling.T
    system = (
        diag_t[:, :, None] * eye_mask
        + couple_t[:, :, None] * follow
        + couple_t[:, None, :] * follow.T
    )
    factor = jnp.linalg.cholesky(system)
    inverse = jax.scipy.linalg.cho_solve((factor, True), jnp.broadcast_to(eye_mask, system.shape))
    return jnp.einsum("bqp,pbx->qbx", inverse, rhs_sum, precision=HIGHEST)


def spike_columns(inverse, edges):
    block_len = inverse.shape[-1]
    leading = (jnp.arange(block_len) == 0).astype(jnp.float32)
    spike_first = edges[:, 0:1] * inverse[:, :, 1] + leading[None, :]
    spike_last = edges[:, block_len - 1 : block_len] * inverse[:, :, block_len - 1]
    return (spike_first, spike_last)


def lon_blocks_solve(blocks, edges):
    block_len = blocks.shape[1]
    unit_base = jnp.ones_like(edges)
    inverse = block_inverse(edges, unit_base)
    interior = jnp.einsum("bij,bjx->bix", inverse, blocks, precision=HIGHEST)
    values = interface_values(
        inverse, edges, unit_base, interior[:, 1], interior[:, block_len - 1], blocks[:, 0]
    )
    return (inverse, interior, values)


def lon_finish(interior, inverse, edges, sep_own, sep_next):
    spike_first, spike_last = spike_columns(inverse, edges)
    return (
        interior
        + spike_first[:, :, None] * sep_own[:, None, :]
        + spike_last[:, :, None] * sep_next[:, None, :]
    )


def longitude_split(weighted, lon_diffusion):
    inverse, interior, values = lon_blocks_solve(weighted, lon_diffusion)
    own_diag, next_diag, coupling, own_rhs, next_rhs = values
    prior_rhs = shifted(next_rhs, "lon", 1)
    gathered = (
        collect(own_diag[None], "lon", 0),
        collect(next_diag[None], "lon", 0),
        collect(coupling[None], "lon", 0),
        collect((own_rhs + prior_rhs)[None], "lon", 0),
    )
    diag_sum = gathered[0] + jnp.roll(gathered[1], 1, axis=0)
    separators = interface_solve(diag_sum, gathered[2], gathered[3])
    part_count = lax.axis_size("lon")
    cycle_pos = lax.axis_index("lon")
    sep_own = lax.dynamic_index_in_dim(separators, cycle_pos, 0, keepdims=False)
    sep_next = lax.dynamic_index_in_dim(separators, (cycle_pos + 1) % part_count, 0, keepdims=False)
    return lon_finish(interior, inverse, lon_diffusion, sep_own, sep_next)


def latitude_split(along_lon, lat_diffusion):
    part_count = lax.axis_size("lat")
    band_pos = lax.axis_index("lat")
    block_len = along_lon.shape[0]
    lat_total = part_count * block_len
    global_rows = band_pos * block_len + jnp.arange(block_len, dtype=jnp.int32)
    latitude = -jnp.pi / 2 + (global_rows.astype(jnp.float32) + 0.5) * jnp.pi / lat_total
    cosine = jnp.cos(latitude)
    edge_keep = (global_rows < lat_total - 1).astype(jnp.float32)
    edges = jnp.transpose(lat_diffusion * edge_keep[:, None])
    base_vals = jnp.broadcast_to(cosine[None, :], edges.shape)
    inverse = block_inverse(edges, base_vals)
    interior = jnp.einsum("bij,jbx->ibx", inverse, along_lon, precision=HIGHEST)
    values = interface_values(
        inverse, edges, base_vals, interior[1], interior[block_len - 1], along_lon[0]
    )
    own_diag, next_diag, coupling, own_rhs, next_rhs = values
    prior_rhs = shifted_2(next_rhs, "lat", 1)
    gathered = (
        collect(own_diag[None], "lat", 0),
        collect(next_diag[None], "lat", 0),
        collect(coupling[None], "lat", 0),
        collect((own_rhs + prior_rhs)[None], "lat", 0),
    )
    diag_sum = gathered[0] + jnp.roll(gathered[1], 1, axis=0)
    separators = interface_solve(diag_sum, gathered[2], gathered[3])
    sep_own = lax.dynamic_index_in_dim(separators, band_pos, 0, keepdims=False)
    sep_next = lax.dynamic_index_in_dim(separators, (band_pos + 1) % part_count, 0, keepdims=False)
    spike_first, spike_last = spike_columns(inverse, edges)
    solved = (
        interior
        + spike_first.T[:, :, None] * sep_own[None]
        + spike_last.T[:, :, None] * sep_next[None]
    )
    return cosine[:, None, None] * solved


def shards(
    ensemble, grad_increment, normalization, lon_diffusion, lat_diffusion, vert_diag, vert_sub
):
    lat_rows, lon_cols, members, levels = ensemble.shape
    weighted = normalization[:, :, None, None] * ensemble * grad_increment[:, :, None, :]
    weighted = weighted.reshape(lat_rows, lon_cols, members * levels)
    along_lon = longitude_split(weighted, lon_diffusion)
    along_lat = latitude_split(along_lon, lat_diffusion)
    along_lat = along_lat.reshape(lat_rows, lon_cols, members, levels)
    factor = jnp.diag(vert_diag) + jnp.diag(vert_sub, -1)
    identity = jnp.eye(levels, dtype=jnp.float32)
    vert_inv = jax.scipy.linalg.cho_solve((factor, True), identity)
    return jnp.einsum("abml,lk->abmk", along_lat, vert_inv, precision=HIGHEST)


def solution(mesh):
    in_specs = (
        P("lat", "lon", None, None),
        P("lat", "lon", None),
        P("lat", "lon"),
        P("lat", "lon"),
        P("lat", "lon"),
        P(),
        P(),
    )
    out_specs = P("lat", "lon", None, None)
    return jax.shard_map(shards, mesh=mesh, in_specs=in_specs, out_specs=out_specs, check_vma=False)
```

profile of v0, /device:TPU:1, one launch (start us, length us, event | category | flops | bytes accessed | tf_op | source)
XLA Modules:
  0.0 387.6 jit_solution(13299793450974717689)
XLA Ops:
  0.2 0.8 negate_select_fusion
  1.3 0.3 fusion.12
  1.6 52.8 %custom-call.55 = f32[48,12,12]{2,1,0:T(8,128)S(1)} custom-call(f32[48,12,12]{2,1,0:T(8,128)S(1)} %fusion.12), custom_call_target="Cholesky" | custom-call | tf_op jit(solution)/shard_map/jit(cholesky)/cholesky | solution.py:51
  54.4 0.2 copy.180
  54.8 1.6 custom-call.56
  56.4 0.3 copy.183
  56.7 0.8 fusion.26
  57.5 0.5 convolution_subtract_fusion
  58.1 1.4 slice_reduce_fusion
  59.5 0.6 broadcast_in_dim.193
  60.1 6.5 %all-to-all-start.6 = ((f32[8,1,48]{2,1,0:T(1,128)}), f32[8,1,48]{2,1,0:T(1,128)S(1)}, u32[]{:S(2)}, u32[]{:S(2)}) async-start(f32[8,1,48]{2,1,0:T(1,128)} %broadcast_in_dim.193), calls=%async_computation.6 | async-start | bytes 8192 | tf_op jit(solution)/shard_map/all_to_all | solution.py:23
  66.6 0.2 slice_reduce_fusion.4
  67.1 0.2 fusion.14
  67.3 52.8 %custom-call.51 = f32[12,48,48]{2,1,0:T(8,128)S(1)} custom-call(f32[12,48,48]{2,1,0:T(8,128)S(1)} %fusion.14), custom_call_target="Cholesky" | custom-call | tf_op jit(solution)/shard_map/jit(cholesky)/cholesky | solution.py:51
  120.4 44.3 %custom-call.52 = f32[12,1,48,48]{2,3,1,0:T(8,128)S(1)} custom-call(f32[12,1,48,48]{3,2,1,0:T(8,128)S(1)} %select_bitcast_fusion), custom_call_target="InvertDiagBlocksLowerTriangular" | custom-call | tf_op jit(solution)/shard_map/jit(_cho_solve)/vmap()/triangular_solve | solution.py:53
  164.6 1.4 fusion.16
  166.0 1.7 multiply_multiply_fusion
  167.7 0.5 reshape.631
  168.2 1.6 convolution_subtract_fusion.1
  169.8 1.2 fusion.67
  171.1 0.8 collective-permute-start
  172.0 0.3 slice_reduce_fusion.5
  172.6 9.8 %custom-call.59 = f32[1,128,128]{1,2,0:T(8,128)S(1)} custom-call(f32[1,128,128]{2,1,0:T(8,128)S(1)} %add_select_fusion), custom_call_target="InvertDiagBlocksLowerTriangular" | custom-call | tf_op jit(solution)/shard_map/jit(_cho_solve)/triangular_solve | solution.py:183
  182.4 0.2 fusion.37
  182.7 0.2 convolution_bitcast_fusion
  183.5 0.6 broadcast_in_dim.194
  184.1 5.1 %all-to-all-start.7 = ((f32[8,1,48]{2,1,0:T(1,128)}), f32[8,1,48]{2,1,0:T(1,128)S(1)}, u32[]{:S(2)}, u32[]{:S(2)}) async-start(f32[8,1,48]{2,1,0:T(1,128)} %broadcast_in_dim.194), calls=%async_computation.7 | async-start | bytes 8192 | tf_op jit(solution)/shard_map/all_to_all | solution.py:23
  189.2 4.5 %all-to-all-done.7 = f32[8,1,48]{2,1,0:T(1,128)S(1)} async-done(((f32[8,1,48]{2,1,0:T(1,128)}), f32[8,1,48]{2,1,0:T(1,128)S(1)}, u32[]{:S(2)}, u32[]{:S(2)}) %all-to-all-start.7) | async-done | bytes 1568 | tf_op jit(solution)/shard_map/all_to_all | solution.py:23
  193.7 0.6 broadcast_in_dim.192
  194.3 3.9 %all-to-all-start.5 = ((f32[8,1,48]{2,1,0:T(1,128)}), f32[8,1,48]{2,1,0:T(1,128)S(1)}, u32[]{:S(2)}, u32[]{:S(2)}) async-start(f32[8,1,48]{2,1,0:T(1,128)} %broadcast_in_dim.192), calls=%async_computation.5 | async-start | bytes 8192 | tf_op jit(solution)/shard_map/all_to_all | solution.py:23
  198.3 4.4 %all-to-all-done.5 = f32[8,1,48]{2,1,0:T(1,128)S(1)} async-done(((f32[8,1,48]{2,1,0:T(1,128)}), f32[8,1,48]{2,1,0:T(1,128)S(1)}, u32[]{:S(2)}, u32[]{:S(2)}) %all-to-all-start.5) | async-done | bytes 1568 | tf_op jit(solution)/shard_map/all_to_all | solution.py:23
  202.7 0.6 broadcast_in_dim.184
  203.3 10.9 %all-to-all-start.3 = ((f32[32,1,12]{2,1,0:T(1,128)}), f32[32,1,12]{2,1,0:T(1,128)S(1)}, u32[]{:S(2)}, u32[]{:S(2)}) async-start(f32[32,1,12]{2,1,0:T(1,128)} %broadcast_in_dim.184), calls=%async_computation.3 | async-start | bytes 32768 | tf_op jit(solution)/shard_map/all_to_all | solution.py:23
  214.3 0.2 fusion.21
  214.5 35.2 %custom-call.57 = f32[48,8,8]{2,1,0:T(8,128)S(1)} custom-call(f32[48,8,8]{2,1,0:T(8,128)S(1)} %fusion.21), custom_call_target="Cholesky" | custom-call | tf_op jit(solution)/shard_map/jit(cholesky)/cholesky | solution.py:83
  249.9 0.6 broadcast_in_dim.112
  250.5 9.2 %all-to-all-start.2 = ((f32[32,1,12]{2,1,0:T(1,128)}), f32[32,1,12]{2,1,0:T(1,128)S(1)}, u32[]{:S(2)}, u32[]{:S(2)}) async-start(f32[32,1,12]{2,1,0:T(1,128)} %broadcast_in_dim.112), calls=%async_computation.2 | async-start | bytes 32768 | tf_op jit(solution)/shard_map/all_to_all | solution.py:23
  259.9 8.3 %all-to-all-done.2 = f32[32,1,12]{2,1,0:T(1,128)S(1)} async-done(((f32[32,1,12]{2,1,0:T(1,128)}), f32[32,1,12]{2,1,0:T(1,128)S(1)}, u32[]{:S(2)}, u32[]{:S(2)}) %all-to-all-start.2) | async-done | bytes 1568 | tf_op jit(solution)/shard_map/all_to_all | solution.py:23
  268.3 0.6 broadcast_in_dim.106
  268.9 3.8 all-to-all-start.1
  272.9 8.3 %all-to-all-done.1 = f32[32,1,12]{2,1,0:T(1,128)S(1)} async-done(((f32[32,1,12]{2,1,0:T(1,128)}), f32[32,1,12]{2,1,0:T(1,128)S(1)}, u32[]{:S(2)}, u32[]{:S(2)}) %all-to-all-start.1) | async-done | bytes 1568 | tf_op jit(solution)/shard_map/all_to_all | solution.py:23
  281.2 1.3 broadcast_in_dim.105
  282.5 3.9 %all-to-all-start = ((f32[32,1,12,512]{3,1,2,0:T(1,128)}), f32[32,1,12,512]{3,1,2,0:T(1,128)S(1)}, u32[]{:S(2)}, u32[]{:S(2)}) async-start(f32[32,1,12,512]{3,1,2,0:T(1,128)} %broadcast_in_dim.105), calls=%async_computation | async-start | bytes 1572864 | tf_op jit(solution)/shard_map/all_to_all | solution.py:23
  286.7 0.2 fusion.19
  286.9 35.2 %custom-call.53 = f32[12,32,32]{2,1,0:T(8,128)S(1)} custom-call(f32[12,32,32]{2,1,0:T(8,128)S(1)} %fusion.19), custom_call_target="Cholesky" | custom-call | tf_op jit(solution)/shard_map/jit(cholesky)/cholesky | solution.py:83
  322.3 29.6 %custom-call.54 = f32[12,1,32,32]{2,3,1,0:T(8,128)S(1)} custom-call(f32[12,1,32,32]{3,2,1,0:T(8,128)S(1)} %select_bitcast_fusion.1), custom_call_target="InvertDiagBlocksLowerTriangular" | custom-call | tf_op jit(solution)/shard_map/jit(_cho_solve)/vmap()/triangular_solve | solution.py:84
  351.9 0.5 fusion.24
  352.4 0.3 fusion.22
  352.7 1.1 fusion.7
  353.9 0.3 multiply_add_fusion
  354.2 2.4 fusion
  356.5 0.7 copy.257
  357.3 6.1 %collective-permute-start.1 = (f32[48,512]{1,0:T(8,128)S(1)}, f32[48,512]{1,0:T(8,128)S(1)}, u32[]{:S(2)}, u32[]{:S(2)}) collective-permute-start(f32[48,512]{1,0:T(8,128)S(1)} %fusion.29), channel_id=1, source_target_pairs={{0,32},{32,64},{64,96},{96,128},{128,160},{160,192},{192,224},{1,3... | collective-permute-start | bytes 294920 | tf_op jit(solution)/shard_map/ppermute | solution.py:33
  363.5 1.4 collective-permute-done.1
  364.9 1.0 broadcast_in_dim.189
  365.9 4.7 %all-to-all-start.4 = ((f32[8,1,48,512]{3,2,1,0:T(8,128)}), f32[8,1,48,512]{3,2,1,0:T(8,128)S(1)}, u32[]{:S(2)}, u32[]{:S(2)}) async-start(f32[8,1,48,512]{3,2,1,0:T(8,128)} %broadcast_in_dim.189), calls=%async_computation.4 | async-start | bytes 1572864 | tf_op jit(solution)/shard_map/all_to_all | solution.py:23
  370.6 0.7 custom-call.58
  371.5 0.6 fusion.33
  372.0 0.5 fusion.68
  372.5 10.4 %all-to-all-done.4 = f32[8,1,48,512]{3,2,1,0:T(8,128)S(1)} async-done(((f32[8,1,48,512]{3,2,1,0:T(8,128)}), f32[8,1,48,512]{3,2,1,0:T(8,128)S(1)}, u32[]{:S(2)}, u32[]{:S(2)}) %all-to-all-start.4) | async-done | bytes 786464 | tf_op jit(solution)/shard_map/all_to_all | solution.py:23
  382.9 1.2 fusion.5
  384.1 0.2 constant_dynamic-slice_fusion.1
  384.3 1.8 fusion.2
  386.2 1.5 copy.201
  (98 shorter events, 4.0 us)
Async XLA Ops:
  56.7 9.9 %copy-start.1 = (f32[12,48]{1,0:T(8,128)S(1)}, f32[12,48]{1,0:T(8,128)}, u32[]{:S(2)}) copy-start(f32[12,48]{1,0:T(8,128)} %param.10) | copy-start | bytes 6916
  58.0 108.0 %copy-start = (f32[12,48,4,128]{3,2,1,0:T(4,128)S(1)}, f32[12,48,4,128]{3,2,1,0:T(4,128)}, u32[]{:S(2)}) copy-start(f32[12,48,4,128]{3,2,1,0:T(4,128)} %param.7) | copy-start | bytes 3538948
  58.0 108.0 %copy-start.2 = (f32[12,48]{1,0:T(8,128)S(1)}, f32[12,48]{1,0:T(8,128)}, u32[]{:S(2)}) copy-start(f32[12,48]{1,0:T(8,128)} %param.9) | copy-start | bytes 6916
  60.1 123.4 %all-to-all-start.6 = ((f32[8,1,48]{2,1,0:T(1,128)}), f32[8,1,48]{2,1,0:T(1,128)S(1)}, u32[]{:S(2)}, u32[]{:S(2)}) async-start(f32[8,1,48]{2,1,0:T(1,128)} %broadcast_in_dim.193), calls=%async_computation.6 | async-start | bytes 8192 | tf_op jit(solution)/shard_map/all_to_all | solution.py:23
  169.8 2.6 copy-start.4
  169.8 2.7 copy-start.3
  171.1 101.7 %collective-permute-start = (f32[12,512]{1,0:T(8,128)S(1)}, f32[12,512]{1,0:T(8,128)S(1)}, u32[]{:S(2)}, u32[]{:S(2)}) collective-permute-start(f32[12,512]{1,0:T(8,128)S(1)} %bitcast_multiply_fusion), channel_id=1, source_target_pairs={{0,1},{1,2},{2,3},{3,4},{4,5},{5,6},{6,7},{7,8},{8,9},{9,10},{10,1... | collective-permute-start | bytes 73736 | tf_op jit(solution)/shard_map/ppermute | solution.py:12
  184.1 9.6 %all-to-all-start.7 = ((f32[8,1,48]{2,1,0:T(1,128)}), f32[8,1,48]{2,1,0:T(1,128)S(1)}, u32[]{:S(2)}, u32[]{:S(2)}) async-start(f32[8,1,48]{2,1,0:T(1,128)} %broadcast_in_dim.194), calls=%async_computation.7 | async-start | bytes 8192 | tf_op jit(solution)/shard_map/all_to_all | solution.py:23
  194.3 8.4 %all-to-all-start.5 = ((f32[8,1,48]{2,1,0:T(1,128)}), f32[8,1,48]{2,1,0:T(1,128)S(1)}, u32[]{:S(2)}, u32[]{:S(2)}) async-start(f32[8,1,48]{2,1,0:T(1,128)} %broadcast_in_dim.192), calls=%async_computation.5 | async-start | bytes 8192 | tf_op jit(solution)/shard_map/all_to_all | solution.py:23
  203.3 46.6 %all-to-all-start.3 = ((f32[32,1,12]{2,1,0:T(1,128)}), f32[32,1,12]{2,1,0:T(1,128)S(1)}, u32[]{:S(2)}, u32[]{:S(2)}) async-start(f32[32,1,12]{2,1,0:T(1,128)} %broadcast_in_dim.184), calls=%async_computation.3 | async-start | bytes 32768 | tf_op jit(solution)/shard_map/all_to_all | solution.py:23
  250.5 17.7 %all-to-all-start.2 = ((f32[32,1,12]{2,1,0:T(1,128)}), f32[32,1,12]{2,1,0:T(1,128)S(1)}, u32[]{:S(2)}, u32[]{:S(2)}) async-start(f32[32,1,12]{2,1,0:T(1,128)} %broadcast_in_dim.112), calls=%async_computation.2 | async-start | bytes 32768 | tf_op jit(solution)/shard_map/all_to_all | solution.py:23
  268.9 12.4 %all-to-all-start.1 = ((f32[32,1,12]{2,1,0:T(1,128)}), f32[32,1,12]{2,1,0:T(1,128)S(1)}, u32[]{:S(2)}, u32[]{:S(2)}) async-start(f32[32,1,12]{2,1,0:T(1,128)} %broadcast_in_dim.106), calls=%async_computation.1 | async-start | bytes 32768 | tf_op jit(solution)/shard_map/all_to_all | solution.py:23
  282.5 70.2 %all-to-all-start = ((f32[32,1,12,512]{3,1,2,0:T(1,128)}), f32[32,1,12,512]{3,1,2,0:T(1,128)S(1)}, u32[]{:S(2)}, u32[]{:S(2)}) async-start(f32[32,1,12,512]{3,1,2,0:T(1,128)} %broadcast_in_dim.105), calls=%async_computation | async-start | bytes 1572864 | tf_op jit(solution)/shard_map/all_to_all | solution.py:23
  357.3 7.5 %collective-permute-start.1 = (f32[48,512]{1,0:T(8,128)S(1)}, f32[48,512]{1,0:T(8,128)S(1)}, u32[]{:S(2)}, u32[]{:S(2)}) collective-permute-start(f32[48,512]{1,0:T(8,128)S(1)} %fusion.29), channel_id=1, source_target_pairs={{0,32},{32,64},{64,96},{96,128},{128,160},{160,192},{192,224},{1,3... | collective-permute-start | bytes 294920 | tf_op jit(solution)/shard_map/ppermute | solution.py:33
  365.9 17.0 %all-to-all-start.4 = ((f32[8,1,48,512]{3,2,1,0:T(8,128)}), f32[8,1,48,512]{3,2,1,0:T(8,128)S(1)}, u32[]{:S(2)}, u32[]{:S(2)}) async-start(f32[8,1,48,512]{3,2,1,0:T(8,128)} %broadcast_in_dim.189), calls=%async_computation.4 | async-start | bytes 1572864 | tf_op jit(solution)/shard_map/all_to_all | solution.py:23
where the time goes:
time: 388 us
  other arithmetic  268 us (69%)
  starting transfers between devices  54.9 us (14%)
  waiting for transfers between devices  37.4 us (10%)
  matrix products  14.2 us (4%)
  local copies, waits for them, and re-layouts  12.6 us (3%)
    another operation x8, other arithmetic, block_inverse(): factor = jnp.linalg.cholesky(matrix)  106 us
    another operation x8, other arithmetic, interface_solve(): factor = jnp.linalg.cholesky(system)  70.6 us
    all_to_all x8, starting transfers between devices, sent_to_all(): return lax.all_to_all(copies, axis, split_axis=0, concat_axis=0, tiled=True)  48 us
    another operation x6, other arithmetic, block_inverse(): inverse = jax.scipy.linalg.cho_solve((factor, True), identity)  46.1 us
    all_to_all x8, waiting for transfers between devices, sent_to_all(): return lax.all_to_all(copies, axis, split_axis=0, concat_axis=0, tiled=True)  36 us
    another operation x6, other arithmetic, interface_solve(): jax.scipy.linalg.cho_solve((factor, True), jnp.broadcast_to(eye_mask, sys...  30.4 us
    another operation x2, other arithmetic, shards(): vert_inv = jax.scipy.linalg.cho_solve((factor, True), identity)  9.92 us
  transfers between devices with their start and end apart: 10, of which 6 were waited for; matrix products, arithmetic and copies ran while one was open for 58% of the time, Pallas kernels for 0%

commit v1 on v0

v1 whole, which is shorter than its diff:
```python
import functools
import math

import jax
import jax.numpy as jnp
from jax import lax
from jax.experimental import pallas as pl
from jax.experimental.pallas import tpu as pltpu
from jax.sharding import PartitionSpec as P

HIGHEST = lax.Precision.HIGHEST
MESH = pl.DeviceIdType.MESH
F32 = jnp.float32

ROWS, COLS, MEMB, LEV = 12, 48, 4, 128
BANDS, BLOCKS = 8, 32
SUB = 8
RUN = COLS // SUB
UNITS = MEMB * RUN
SHARE = UNITS // BANDS
NLAT = ROWS * BANDS
HALF = SHARE * SUB


def solver_of(row, core):
    return ((2 * row + core) * 4) // 3


def rows_at(start, count=SUB):
    return pl.ds(pl.multiple_of(start, SUB), count)


def wide(row, rows=SUB):
    return jnp.broadcast_to(row, (rows, LEV))


def sublane_sums(vals):
    sub = lax.broadcasted_iota(jnp.int32, (SUB, LEV), 0)
    low = sub < 4
    four = [
        jnp.where(low, vals[k], vals[k + 4]) + pltpu.roll(jnp.where(low, vals[k + 4], vals[k]), 4, 0)
        for k in range(4)
    ]
    low = sub % 4 < 2
    two = [
        jnp.where(low, four[k] + pltpu.roll(four[k], 6, 0), four[k + 2] + pltpu.roll(four[k + 2], 2, 0))
        for k in range(2)
    ]
    low = sub % 2 < 1
    return jnp.where(low, two[0] + pltpu.roll(two[0], 7, 0), two[1] + pltpu.roll(two[1], 1, 0))


def sums_before(val):
    sub = lax.broadcasted_iota(jnp.int32, (SUB, LEV), 0)
    val = jnp.where(sub >= 1, pltpu.roll(val, 1, 0), 0.0)
    for step in (1, 2, 4):
        val = val + jnp.where(sub >= step, pltpu.roll(val, step, 0), 0.0)
    return val


def sums_after(val):
    sub = lax.broadcasted_iota(jnp.int32, (SUB, LEV), 0)
    val = jnp.where(sub < SUB - 1, pltpu.roll(val, SUB - 1, 0), 0.0)
    for step in (1, 2, 4):
        val = val + jnp.where(sub < SUB - step, pltpu.roll(val, SUB - step, 0), 0.0)
    return val


def kernel(
    e_hbm, g_hbm, norm_ref, lon_ref, lat_ref, diag_ref, below_ref, out_hbm,
    e_v, g_v, out_v, y_v,
    tmp, rk_t, phi_t, w1_t, n_t, phin_t, w1n_t,
    w1n_e, phin_e, w1_e, phi_e,
    lat_pad, lat_rk, lat_rows, lat_t, w1l_e, phil_e, cw1_e, cphi_e,
    vinv,
    cs_a, cr_a, ss_a, sr_a, ts_a, tr_a, rows_a, inv_a,
    cs_b, cr_b, ss_b, sr_b, ts_b, tr_b, rows_b, tb_b, el_b,
    load_sem, store_sem,
    ca_send, ca_recv, sa_send, sa_recv, ta_send, ta_recv,
    cb_send, cb_recv, sb_send, sb_recv, tb_send, tb_recv,
):
    band = lax.axis_index("lat")
    me = lax.axis_index("lon")
    core = band % 2
    place = me - me // 4
    is_solver = jnp.logical_and(me % 4 != 3, place % 2 == core)
    my_row = place // 2

    loads = [
        pltpu.make_async_copy(g_hbm, g_v, load_sem.at[0]),
        pltpu.make_async_copy(e_hbm, e_v, load_sem.at[1]),
    ]
    for copy in loads:
        copy.start()

    barrier = pltpu.get_barrier_semaphore()

    def greet_lon(step, _):
        pl.semaphore_signal(barrier, inc=1, device_id=(band, (me + step) % BLOCKS), device_id_type=MESH)
        return 0

    def greet_lat(step, _):
        pl.semaphore_signal(barrier, inc=1, device_id=((band + step) % BANDS, me), device_id_type=MESH)
        return 0

    lax.fori_loop(1, BLOCKS, greet_lon, 0)
    lax.fori_loop(1, BANDS, greet_lat, 0)

    tmp[...] = jnp.full((LEV, LEV), 2048.0, F32)
    tmp[0:ROWS, 0:COLS] = lon_ref[...]
    rk_t[...] = 1.0 / tmp[...].T[0:COLS]
    tmp[0:ROWS, 0:COLS] = norm_ref[...]
    n_t[...] = tmp[...].T[0:COLS]
    flow_p = jnp.zeros((1, LEV), F32)
    flow_s = jnp.zeros((1, LEV), F32)
    val_p = rk_t[0:1]
    val_s = rk_t[COLS - 1 : COLS]
    phi_t[0:1] = jnp.zeros((1, LEV), F32)
    phi_t[1:2] = val_p
    w1_t[COLS - 1 : COLS] = val_s
    for i in range(1, COLS):
        flow_p = flow_p + val_p
        val_p = val_p + (1.0 + flow_p) * rk_t[i : i + 1]
        if i < COLS - 1:
            phi_t[i + 1 : i + 2] = val_p
        k = COLS - i
        flow_s = flow_s + val_s
        val_s = val_s + (1.0 + flow_s) * rk_t[k - 1 : k]
        w1_t[k - 1 : k] = val_s
    edge = 1.0 / val_p
    scale = 1.0 / val_s
    cs_a[...] = jnp.zeros((SUB, LEV), F32)
    cs_a[0:1] = edge
    cs_a[1:2] = 1.0 + flow_s * scale
    cs_a[2:3] = flow_p * edge
    w1_t[...] = w1_t[...] * scale
    w1n_t[...] = w1_t[...] * n_t[...]
    phin_t[...] = phi_t[...] * n_t[...]

    pl.semaphore_wait(barrier, BLOCKS + BANDS - 2)

    def coeff_copy_a(row):
        return pltpu.make_async_remote_copy(
            src_ref=cs_a,
            dst_ref=cr_a.at[rows_at(me * SUB)],
            send_sem=ca_send.at[row],
            recv_sem=ca_recv,
            device_id=(band, solver_of(row, core)),
            device_id_type=MESH,
        )

    def rhs_copy_a(row):
        return pltpu.make_async_remote_copy(
            src_ref=ss_a.at[rows_at(row * SUB)],
            dst_ref=sr_a.at[rows_at(me * SUB)],
            send_sem=sa_send.at[row],
            recv_sem=sa_recv,
            device_id=(band, solver_of(row, core)),
            device_id_type=MESH,
        )

    def back_copy_a(target):
        return pltpu.make_async_remote_copy(
            src_ref=ts_a.at[rows_at(target * SUB)],
            dst_ref=tr_a.at[rows_at(my_row * SUB)],
            send_sem=ta_send.at[target],
            recv_sem=ta_recv.at[my_row],
            device_id=(band, target),
            device_id_type=MESH,
        )

    def copy_b(kind, target):
        size = SUB if kind == 0 else 2 * HALF
        source = (cs_b, ss_b, ts_b)[kind]
        dest = (cr_b, sr_b, tr_b)[kind]
        return pltpu.make_async_remote_copy(
            src_ref=source if kind == 0 else source.at[rows_at(target * size, size)],
            dst_ref=dest.at[rows_at(band * size, size)],
            send_sem=(cb_send, sb_send, tb_send)[kind].at[target],
            recv_sem=(cb_recv, sb_recv, tb_recv)[kind].at[band],
            device_id=(target, me),
            device_id_type=MESH,
        )

    def landed_b(kind, source):
        size = SUB if kind == 0 else 2 * HALF
        dest = (cr_b, sr_b, tr_b)[kind]
        slot = dest.at[rows_at(source * size, size)]
        return pltpu.make_async_copy(slot, slot, (cb_recv, sb_recv, tb_recv)[kind].at[source])

    def send_coeff_a(step, _):
        row = (me + step) % ROWS

        @pl.when(solver_of(row, core) != me)
        def _():
            coeff_copy_a(row).start()

        return 0

    lax.fori_loop(0, ROWS, send_coeff_a, 0)

    @pl.when(is_solver)
    def _():
        cr_a[rows_at(me * SUB)] = cs_a[...]

    lat_pad[...] = jnp.full((16, LEV), 512.0, F32)
    lat_pad[0:ROWS, 0:COLS] = lat_ref[...]
    lat_rk[...] = 1.0 / lat_pad[...]
    at = band * ROWS + lax.broadcasted_iota(jnp.int32, (16, LEV), 0)
    at = jnp.minimum(at, NLAT - 1 - at).astype(F32)
    angle = (at + 0.5) * (math.pi / NLAT)
    square = angle * angle
    series = jnp.full((16, LEV), 1.0 / math.factorial(13), F32)
    for power in (11, 9, 7, 5, 3, 1):
        series = 1.0 / math.factorial(power) - series * square
    lat_t[0:16] = angle * series

    def cosine(j):
        return lat_t[j : j + 1]

    last = jnp.where(band == BANDS - 1, 0.0, 1.0) * lat_pad[ROWS - 1 : ROWS]
    lat_rows[...] = jnp.zeros((LEV, LEV), F32)
    flow_p = jnp.zeros((1, LEV), F32)
    flow_s = jnp.zeros((1, LEV), F32)
    val_p = lat_rk[0:1]
    val_s = jnp.ones((1, LEV), F32)
    lat_rows[17:18] = val_p
    lat_rows[ROWS - 1 : ROWS] = val_s
    for j in range(1, ROWS):
        flow_p = flow_p + cosine(j) * val_p
        if j < ROWS - 1:
            val_p = val_p + (1.0 + flow_p) * lat_rk[j : j + 1]
            lat_rows[17 + j : 18 + j] = val_p
        k = ROWS - j
        flow_s = flow_s + cosine(k) * val_s
        val_s = val_s + (last + flow_s) * lat_rk[k - 1 : k]
        lat_rows[k - 1 : k] = val_s
    edge = last / (last * val_p + 1.0 + flow_p)
    scale = 1.0 / val_s
    cs_b[...] = jnp.zeros((SUB, LEV), F32)
    cs_b[0:1] = edge
    cs_b[1:2] = cosine(0) + flow_s * scale
    cs_b[2:3] = flow_p * edge
    lat_rows[0:16] = lat_rows[0:16] * scale
    lat_rows[32:48] = lat_rows[0:16] * lat_t[0:16]
    lat_rows[48:64] = lat_rows[16:32] * lat_t[0:16]

    def send_coeff_b(step, _):
        copy_b(0, (band + step) % BANDS).start()
        return 0

    lax.fori_loop(1, BANDS, send_coeff_b, 0)
    cr_b[rows_at(band * SUB)] = cs_b[...]

    for t in range(RUN):
        for source, target in ((w1n_t, w1n_e), (phin_t, phin_e)):
            part = source[pl.ds(t, SUB, stride=RUN), :]
            for j in range(ROWS):
                at = j * COLS + t * SUB
                target[at : at + SUB] = jnp.broadcast_to(part[:, j : j + 1], (SUB, LEV))

    for copy in loads:
        copy.wait()

    def contribute(step, _):
        row = (me + step) % ROWS
        sums = [jnp.zeros((SUB, LEV), F32) for _ in range(2 * MEMB)]
        for t in range(RUN):
            grad = g_v[pl.ds(row * COLS + t, SUB, stride=RUN), :]
            first = w1n_e[rows_at(row * COLS + t * SUB)] * grad
            second = phin_e[rows_at(row * COLS + t * SUB)] * grad
            for m in range(MEMB):
                value = e_v[pl.ds(row * COLS * MEMB + t * MEMB + m, SUB, stride=RUN * MEMB), :]
                sums[m] = sums[m] + first * value
                sums[MEMB + m] = sums[MEMB + m] + second * value
        ss_a[rows_at(row * SUB)] = sublane_sums(sums)

        @pl.when(solver_of(row, core) != me)
        def _():
            rhs_copy_a(row).start()

        return 0

    lax.fori_loop(0, ROWS, contribute, 0)

    @pl.when(is_solver)
    def _():
        sr_a[rows_at(me * SUB)] = ss_a[rows_at(my_row * SUB)]

    tmp[0:SUB] = jnp.zeros((SUB, LEV), F32)
    tmp[0:1, 0 : LEV - 1] = below_ref[...]
    dinv = 1.0 / wide(diag_ref[...])
    lane = lax.broadcasted_iota(jnp.int32, (SUB, LEV), 1)
    ratio = jnp.where(lane == 0, 0.0, -pltpu.roll(wide(tmp[0:1]), 1, 1) * dinv)
    row_ids = lax.broadcasted_iota(jnp.int32, (LEV, LEV), 0)
    col_ids = lax.broadcasted_iota(jnp.int32, (LEV, LEV), 1)
    half = jnp.where(row_ids == col_ids, wide(dinv[0:1], LEV), 0.0)
    step = 1
    while step < LEV:
        half = half + wide(ratio[0:1], LEV) * pltpu.roll(half, step, 1)
        ratio = ratio * pltpu.roll(ratio, step, 1)
        step *= 2
    vinv[...] = lax.dot_general(
        half, half, (((1,), (1,)), ((), ())), precision=HIGHEST, preferred_element_type=F32
    )

    @pl.when(is_solver)
    def _():
        slots = cr_a.at[rows_at(0, (BLOCKS - 1) * SUB)]
        pltpu.make_async_copy(slots, slots, ca_recv).wait()
        link = cr_a[pl.ds(0, BLOCKS, stride=SUB), :]
        base = cr_a[pl.ds(1, BLOCKS, stride=SUB), :] + pltpu.roll(cr_a[pl.ds(2, BLOCKS, stride=SUB), :], 1, 0)
        rows_a[0:BLOCKS] = 1.0 / link
        rows_a[BLOCKS : 2 * BLOCKS] = base
        flow_p = jnp.zeros((1, LEV), F32)
        flow_s = jnp.zeros((1, LEV), F32)
        val_p = rows_a[0:1]
        val_s = rows_a[BLOCKS - 1 : BLOCKS]
        tmp[0:1] = jnp.zeros((1, LEV), F32)
        tmp[1:2] = val_p
        tmp[2 * BLOCKS - 1 : 2 * BLOCKS] = val_s
        for p in range(1, BLOCKS):
            flow_p = flow_p + rows_a[BLOCKS + p : BLOCKS + p + 1] * val_p
            val_p = val_p + (1.0 + flow_p) * rows_a[p : p + 1]
            if p < BLOCKS - 1:
                tmp[p + 1 : p + 2] = val_p
            k = BLOCKS - p
            flow_s = flow_s + rows_a[BLOCKS + k : BLOCKS + k + 1] * val_s
            val_s = val_s + (1.0 + flow_s) * rows_a[k - 1 : k]
            tmp[BLOCKS + k - 1 : BLOCKS + k] = val_s
        first = tmp[BLOCKS : 2 * BLOCKS] * (1.0 / val_s)
        both = first + tmp[0:BLOCKS] * (1.0 / val_p)
        total = jnp.sum(both * base, axis=0, keepdims=True)
        tmp[BLOCKS : 2 * BLOCKS] = first
        tmp[2 * BLOCKS : 3 * BLOCKS] = both * (1.0 / total)
        tmp[3 * BLOCKS : 4 * BLOCKS] = both
        whole = tmp[...]
        lanes = lax.broadcasted_iota(jnp.int32, (LEV, LEV), 1)
        column = jnp.sum(jnp.where(lanes == my_row, whole, 0.0), axis=1, keepdims=True)
        column = jnp.broadcast_to(column, (LEV, LEV))
        tmp[...] = whole.T
        line = wide(tmp[pl.ds(my_row, 1), :])
        phi_row = wide(line[0:1], BLOCKS)
        first_row = wide(pltpu.roll(line, LEV - BLOCKS, 1)[0:1], BLOCKS)
        both_row = wide(pltpu.roll(line, LEV - 2 * BLOCKS, 1)[0:1], BLOCKS)
        sub_ids = lax.broadcasted_iota(jnp.int32, (BLOCKS, LEV), 0)
        lane_ids = lax.broadcasted_iota(jnp.int32, (BLOCKS, LEV), 1)
        inv_a[0:BLOCKS] = (
            jnp.where(
                sub_ids <= lane_ids,
                column[0:BLOCKS] * first_row,
                column[BLOCKS : 2 * BLOCKS] * phi_row,
            )
            + column[3 * BLOCKS : 4 * BLOCKS] * both_row
        )
        link = jnp.sum(jnp.where(lane_ids == my_row, link, 0.0), axis=1, keepdims=True)
        inv_a[BLOCKS : 2 * BLOCKS] = jnp.broadcast_to(link, (BLOCKS, LEV))

    @pl.when(is_solver)
    def _():
        slots = sr_a.at[rows_at(0, (BLOCKS - 1) * SUB)]
        pltpu.make_async_copy(slots, slots, sa_recv).wait()
        link = inv_a[BLOCKS : 2 * BLOCKS]
        inverse = inv_a[0:BLOCKS][:, 0:BLOCKS]
        for m in range(MEMB):
            own = sr_a[pl.ds(m, BLOCKS, stride=SUB), :]
            after = sr_a[pl.ds(MEMB + m, BLOCKS, stride=SUB), :]
            rhs = own + pltpu.roll(link * after, 1, 0)
            rhs = jnp.dot(rhs, vinv[...], precision=HIGHEST, preferred_element_type=F32)
            found = jnp.dot(inverse, rhs, precision=HIGHEST, preferred_element_type=F32)
            ts_a[pl.ds(m, BLOCKS, stride=SUB), :] = found
            ts_a[pl.ds(MEMB + m, BLOCKS, stride=SUB), :] = link * pltpu.roll(found, BLOCKS - 1, 0)

        def send_back(step, _):
            back_copy_a((me + step) % BLOCKS).start()
            return 0

        lax.fori_loop(1, BLOCKS, send_back, 0)
        tr_a[rows_at(my_row * SUB)] = ts_a[rows_at(me * SUB)]

    for t in range(RUN):
        for source, target in ((w1_t, w1_e), (phi_t, phi_e)):
            part = source[pl.ds(t, SUB, stride=RUN), :]
            for j in range(ROWS):
                at = j * COLS + t * SUB
                target[at : at + SUB] = jnp.broadcast_to(part[:, j : j + 1], (SUB, LEV))

    def interior(row, _):
        firsts, seconds = [], []
        for t in range(RUN):
            grad = g_v[pl.ds(row * COLS + t, SUB, stride=RUN), :]
            firsts.append(w1n_e[rows_at(row * COLS + t * SUB)] * grad)
            seconds.append(phin_e[rows_at(row * COLS + t * SUB)] * grad)
        for m in range(MEMB):
            values = [
                e_v[pl.ds(row * COLS * MEMB + t * MEMB + m, SUB, stride=RUN * MEMB), :] for t in range(RUN)
            ]
            ahead = [seconds[0] * values[0]]
            for t in range(1, RUN):
                ahead.append(ahead[-1] + seconds[t] * values[t])
            behind = [None] * RUN
            total = jnp.zeros((SUB, LEV), F32)
            for t in reversed(range(RUN)):
                behind[t] = total
                total = total + firsts[t] * values[t]
            before = sums_before(ahead[-1])
            after = sums_after(total)
            for t in range(RUN):
                w1 = w1_e[rows_at(row * COLS + t * SUB)]
                phi = phi_e[rows_at(row * COLS + t * SUB)]
                y_v[rows_at(((m * RUN + t) * ROWS + row) * SUB)] = w1 * (before + ahead[t]) + phi * (
                    after + behind[t]
                )
        return 0

    lax.fori_loop(0, ROWS, interior, 0)

    size = UNITS * SUB

    def vertical(part, _):
        at = rows_at(part * size, size)
        y_v[at] = jnp.dot(y_v[at], vinv[...], precision=HIGHEST, preferred_element_type=F32)
        return 0

    lax.fori_loop(0, ROWS, vertical, 0)

    lat_t[...] = lat_rows[...].T
    for t in range(RUN):
        part = lat_t[pl.ds(t, SUB, stride=RUN), :]
        for number, target in enumerate((w1l_e, phil_e, cw1_e, cphi_e)):
            for j in range(ROWS):
                at = j * COLS + t * SUB
                lane_at = number * 16 + j
                target[at : at + SUB] = jnp.broadcast_to(part[:, lane_at : lane_at + 1], (SUB, LEV))

    def wait_coeff_b(step, _):
        landed_b(0, (band + step) % BANDS).wait()
        return 0

    lax.fori_loop(1, BANDS, wait_coeff_b, 0)
    flow_p = jnp.zeros((1, LEV), F32)
    flow_s = jnp.zeros((1, LEV), F32)
    val_p = jnp.ones((1, LEV), F32)
    val_s = jnp.ones((1, LEV), F32)

    def band_base(p):
        own = cr_b[p * SUB + 1 : p * SUB + 2]
        return own if p == 0 else own + cr_b[(p - 1) * SUB + 2 : (p - 1) * SUB + 3]

    def band_link(p):
        return cr_b[p * SUB : p * SUB + 1]

    rows_b[...] = jnp.zeros((LEV, LEV), F32)
    rows_b[0:1] = val_p
    rows_b[2 * BANDS - 1 : 2 * BANDS] = val_s
    for p in range(BANDS - 1):
        flow_p = flow_p + band_base(p) * val_p
        val_p = val_p + flow_p / band_link(p)
        rows_b[p + 1 : p + 2] = val_p
        k = BANDS - 1 - p
        flow_s = flow_s + band_base(k) * val_s
        val_s = val_s + flow_s / band_link(k - 1)
        rows_b[BANDS + k - 1 : BANDS + k] = val_s
    flow_s = flow_s + band_base(0) * val_s
    rows_b[BANDS : 2 * BANDS] = rows_b[BANDS : 2 * BANDS] * (1.0 / flow_s)
    for p in range(BANDS - 1):
        rows_b[2 * BANDS + p : 2 * BANDS + p + 1] = band_link(p)
    tb_b[...] = rows_b[...].T
    for tt in range(SHARE):
        part = tb_b[pl.ds((band % 2) * SHARE + tt, SUB, stride=RUN), :]
        for number in range(3 * BANDS):
            at = (number * SHARE + tt) * SUB
            el_b[at : at + SUB] = jnp.broadcast_to(part[:, number : number + 1], (SUB, LEV))

    def wait_back_a(row, _):
        @pl.when(solver_of(row, core) != me)
        def _():
            slot = tr_a.at[rows_at(row * SUB)]
            pltpu.make_async_copy(slot, slot, ta_recv.at[row]).wait()

        return 0

    lax.fori_loop(0, ROWS, wait_back_a, 0)

    def finish_lon(step, _):
        share = (band + 1 + step) % BANDS
        m = share // 2
        for tt in range(SHARE):
            t = (share % 2) * SHARE + tt
            own = jnp.zeros((SUB, LEV), F32)
            after = jnp.zeros((SUB, LEV), F32)
            for j in range(ROWS):
                at = rows_at(((share * SHARE + tt) * ROWS + j) * SUB)
                coeff = rows_at(j * COLS + t * SUB)
                sep_own = wide(tr_a[pl.ds(j * SUB + m, 1), :])
                sep_next = wide(tr_a[pl.ds(j * SUB + MEMB + m, 1), :])
                value = y_v[at] + w1_e[coeff] * sep_own + phi_e[coeff] * sep_next
                y_v[at] = value
                own = own + w1l_e[coeff] * value
                after = after + phil_e[coeff] * value
            ss_b[rows_at(share * 2 * HALF + tt * SUB)] = own
            ss_b[rows_at(share * 2 * HALF + HALF + tt * SUB)] = after

        @pl.when(share != band)
        def _():
            copy_b(1, share).start()

        return 0

    lax.fori_loop(0, BANDS, finish_lon, 0)
    sr_b[rows_at(band * 2 * HALF, 2 * HALF)] = ss_b[rows_at(band * 2 * HALF, 2 * HALF)]

    def interior_lat(unit, _):
        t = unit % RUN
        total = jnp.zeros((SUB, LEV), F32)
        aheads = []
        for j in range(ROWS):
            at = rows_at((unit * ROWS + j) * SUB)
            total = total + phil_e[rows_at(j * COLS + t * SUB)] * y_v[at]
            aheads.append(total)
        total = jnp.zeros((SUB, LEV), F32)
        for j in reversed(range(ROWS)):
            at = rows_at((unit * ROWS + j) * SUB)
            coeff = rows_at(j * COLS + t * SUB)
            value = y_v[at]
            y_v[at] = cw1_e[coeff] * aheads[j] + cphi_e[coeff] * total
            total = total + w1l_e[coeff] * value
        return 0

    lax.fori_loop(0, UNITS, interior_lat, 0)

    def wait_rhs_b(step, _):
        landed_b(1, (band + step) % BANDS).wait()
        return 0

    lax.fori_loop(1, BANDS, wait_rhs_b, 0)

    for tt in range(SHARE):

        def spread(number):
            at = (number * SHARE + tt) * SUB
            return el_b[at : at + SUB]

        rhs = []
        total = jnp.zeros((SUB, LEV), F32)
        aheads = []
        for p in range(BANDS):
            at = p * 2 * HALF + tt * SUB
            value = sr_b[at : at + SUB]
            if p > 0:
                before = at - HALF
                value = value + spread(2 * BANDS + p - 1) * sr_b[before : before + SUB]
            rhs.append(value)
            total = total + spread(p) * value
            aheads.append(total)
        total = jnp.zeros((SUB, LEV), F32)
        found = None
        for p in reversed(range(BANDS)):
            at = p * 2 * HALF + tt * SUB
            if p == BANDS - 1:
                ts_b[at + HALF : at + HALF + SUB] = jnp.zeros((SUB, LEV), F32)
            else:
                ts_b[at + HALF : at + HALF + SUB] = spread(2 * BANDS + p) * found
            found = spread(BANDS + p) * aheads[p] + spread(p) * total
            ts_b[at : at + SUB] = found
            total = total + spread(BANDS + p) * rhs[p]

    def send_back_b(step, _):
        copy_b(2, (band + step) % BANDS).start()
        return 0

    lax.fori_loop(1, BANDS, send_back_b, 0)
    tr_b[rows_at(band * 2 * HALF, 2 * HALF)] = ts_b[rows_at(band * 2 * HALF, 2 * HALF)]

    def finish(step, _):
        share = (band + step) % BANDS

        @pl.when(share != band)
        def _():
            landed_b(2, share).wait()

        m = share // 2
        for tt in range(SHARE):
            t = (share % 2) * SHARE + tt
            sep_own = tr_b[rows_at(share * 2 * HALF + tt * SUB)]
            sep_next = tr_b[rows_at(share * 2 * HALF + HALF + tt * SUB)]
            for j in range(ROWS):
                at = rows_at(((share * SHARE + tt) * ROWS + j) * SUB)
                coeff = rows_at(j * COLS + t * SUB)
                out_v[pl.ds(j * COLS * MEMB + t * MEMB + m, SUB, stride=RUN * MEMB), :] = (
                    y_v[at] + cw1_e[coeff] * sep_own + cphi_e[coeff] * sep_next
                )
        return 0

    lax.fori_loop(0, BANDS, finish, 0)
    result = pltpu.make_async_copy(out_v, out_hbm, store_sem)
    result.start()

    def sent_a(row, _):
        @pl.when(solver_of(row, core) != me)
        def _():
            coeff_copy_a(row).wait_send()
            rhs_copy_a(row).wait_send()

        return 0

    lax.fori_loop(0, ROWS, sent_a, 0)

    @pl.when(is_solver)
    def _():
        def sent_back(step, _):
            back_copy_a((me + step) % BLOCKS).wait_send()
            return 0

        lax.fori_loop(1, BLOCKS, sent_back, 0)

    def sent_b(step, _):
        for kind in range(3):
            copy_b(kind, (band + step) % BANDS).wait_send()
        return 0

    lax.fori_loop(1, BANDS, sent_b, 0)
    result.wait()


def shards(
    ensemble, grad_increment, normalization, lon_diffusion, lat_diffusion, vert_diag, vert_sub
):
    block = ROWS * COLS * MEMB
    vmem = pl.BlockSpec(memory_space=pltpu.VMEM)
    anywhere = pl.BlockSpec(memory_space=pl.ANY)

    def buf(rows):
        return pltpu.VMEM((rows, LEV), F32)

    coeffs = ROWS * COLS
    dma = pltpu.SemaphoreType.DMA
    scratch = [
        buf(block), buf(coeffs), buf(block), buf(block),
        buf(LEV), *[buf(COLS)] * 6,
        *[buf(coeffs)] * 4,
        buf(16), buf(16), buf(LEV), buf(LEV), *[buf(coeffs)] * 4,
        buf(LEV),
        buf(SUB), buf(BLOCKS * SUB), buf(ROWS * SUB), buf(BLOCKS * SUB), buf(BLOCKS * SUB), buf(ROWS * SUB),
        buf(2 * BLOCKS), buf(2 * BLOCKS),
        buf(SUB), buf(BANDS * SUB), *[buf(BANDS * 2 * HALF)] * 4,
        buf(LEV), buf(LEV), buf(3 * BANDS * HALF),
        dma((2,)), dma,
        dma((ROWS,)), dma, dma((ROWS,)), dma, dma((BLOCKS,)), dma((ROWS,)),
        *[dma((BANDS,))] * 6,
    ]
    out = pl.pallas_call(
        kernel,
        out_shape=jax.ShapeDtypeStruct((block, LEV), F32),
        in_specs=[anywhere, anywhere, vmem, vmem, vmem, vmem, vmem],
        out_specs=anywhere,
        scratch_shapes=scratch,
        compiler_params=pltpu.CompilerParams(
            collective_id=0, has_side_effects=True, vmem_limit_bytes=32 * 1024 * 1024
        ),
    )(
        ensemble.reshape(block, LEV),
        grad_increment.reshape(coeffs, LEV),
        normalization,
        lon_diffusion,
        lat_diffusion,
        vert_diag.reshape(1, LEV),
        vert_sub.reshape(1, LEV - 1),
    )
    return out.reshape(ROWS, COLS, MEMB, LEV)


def solution(mesh):
    in_specs = (
        P("lat", "lon", None, None),
        P("lat", "lon", None),
        P("lat", "lon"),
        P("lat", "lon"),
        P("lat", "lon"),
        P(),
        P(),
    )
    out_specs = P("lat", "lon", None, None)
    return jax.shard_map(shards, mesh=mesh, in_specs=in_specs, out_specs=out_specs, check_vma=False)
```

time: 388 us -> 44.6 us (0.11)
  other arithmetic: 268 us -> 0 us
  starting transfers between devices: 54.9 us -> 0 us
  Pallas kernels: 0 us -> 37.6 us
  waiting for transfers between devices: 37.4 us -> 0 us
  matrix products: 14.2 us -> 0 us
  local copies, waits for them, and re-layouts: 12.6 us -> 6.65 us
    another operation x30 -> x0, other arithmetic: 263 us -> none  [the longest x8 106 us: block_inverse(): factor = jnp.linalg.cholesky(matrix)]
    all_to_all x8 -> x0, starting transfers between devices: 48 us -> none  [sent_to_all(): return lax.all_to_all(copies, axis, split_axis=0, concat_axis=0, tiled=True)]
    pallas_call x0 -> x1, Pallas kernels: none -> 37.6 us  [shards(): pl.pallas_call(kernel, out_shape=jax.ShapeDtypeStruct((block, LEV), F32),...]
    all_to_all x8 -> x0, waiting for transfers between devices: 36 us -> none  [sent_to_all(): return lax.all_to_all(copies, axis, split_axis=0, concat_axis=0, tiled=True)]
    dot_general x5 -> x0, matrix products: 7.66 us -> none  [the longest x1 2.35 us: latitude_split(): interior = jnp.einsum('bij,jbx->ibx', inverse, along_lon, precision=HIGHEST)]
    ppermute x2 -> x0, starting transfers between devices: 6.95 us -> none  [the longest x1 6.13 us: shifted_2(): lax.ppermute(value, axis, [(source, source + steps) for source in range(i...]
    another operation x10 -> x0, matrix products: 6.53 us -> none  [the longest x4 4.23 us: block_inverse(): inverse = jax.scipy.linalg.cho_solve((factor, True), identity)]
    unnamed x17 -> x15, local copies, waits for them, and re-layouts: 0.15 us -> 6.65 us
  transfers between devices with their start and end apart: 10 -> 0, of which waited for: 6 -> 0; matrix products, arithmetic and copies ran while one was open for 58% -> 0% of each run, Pallas kernels for 0% -> 0%
where the time goes in v1:
time: 44.6 us; the launch traced here: 44.3 us
  Pallas kernels  37.6 us (84%)
  local copies, waits for them, and re-layouts  6.65 us (15%)
    pallas_call x1, Pallas kernels, shards(): pl.pallas_call(kernel, out_shape=jax.ShapeDtypeStruct((block, LEV), F32),...  37.6 us
    unnamed x15, local copies, waits for them, and re-layouts  6.65 us

profile of v1, /device:TPU:1, one launch (start us, length us, event | category | flops | bytes accessed | tf_op | source)
XLA Modules:
  0.0 44.3 jit_solution(8922067701595811271)
XLA Ops:
  0.0 0.0 copy-start
  0.0 1.3 %copy-done = f32[12,48,4,128]{3,2,1,0:T(4,128)S(1)} copy-done((f32[12,48,4,128]{3,2,1,0:T(4,128)S(1)}, f32[12,48,4,128]{3,2,1,0:T(4,128)}, u32[]{:S(2)}) %copy-start) | copy-done | bytes 1179672
  1.3 0.0 copy-start.1
  1.3 1.0 %copy-done.1 = f32[12,48,128]{2,1,0:T(8,128)S(1)} copy-done((f32[12,48,128]{2,1,0:T(8,128)S(1)}, f32[12,48,128]{2,1,0:T(8,128)}, u32[]{:S(2)}) %copy-start.1) | copy-done | bytes 294936
  2.2 0.0 copy-start.2
  2.2 0.7 %copy-done.2 = f32[12,48]{1,0:T(8,128)S(1)} copy-done((f32[12,48]{1,0:T(8,128)S(1)}, f32[12,48]{1,0:T(8,128)}, u32[]{:S(2)}) %copy-start.2) | copy-done | bytes 2328
  2.9 0.0 copy-start.3
  2.9 0.7 %copy-done.3 = f32[12,48]{1,0:T(8,128)S(1)} copy-done((f32[12,48]{1,0:T(8,128)S(1)}, f32[12,48]{1,0:T(8,128)}, u32[]{:S(2)}) %copy-start.3) | copy-done | bytes 2328
  3.6 0.0 copy-start.4
  3.6 0.7 %copy-done.4 = f32[12,48]{1,0:T(8,128)S(1)} copy-done((f32[12,48]{1,0:T(8,128)S(1)}, f32[12,48]{1,0:T(8,128)}, u32[]{:S(2)}) %copy-start.4) | copy-done | bytes 2328
  4.3 0.0 copy-start.5
  4.3 0.7 %copy-done.5 = f32[128]{0:T(128)S(1)} copy-done((f32[128]{0:T(128)S(1)}, f32[128]{0:T(128)}, u32[]{:S(2)}) %copy-start.5) | copy-done | bytes 536
  5.0 0.0 copy-start.6
  5.0 0.7 %copy-done.6 = f32[127]{0:T(128)S(1)} copy-done((f32[127]{0:T(128)S(1)}, f32[127]{0:T(128)}, u32[]{:S(2)}) %copy-start.6) | copy-done | bytes 532
  5.6 37.6 %shard_map.73 = f32[2304,128]{1,0:T(8,128)S(1)} custom-call(f32[2304,128]{1,0:T(8,128)S(1)} %bitcast.6, f32[576,128]{1,0:T(8,128)S(1)} %bitcast.7, f32[12,48]{1,0:T(8,128)S(1)} %copy-done.2, f32[12,48]{1,0:T(8,128)S(1)} %copy-done.3, f32[12,48]{1,0:T(8,128)S(1)} %copy-done.4, f32[1,128]{1,0:T(1,128)S(1)} %bitcast.8, f32[1,127]{1,0:T(1,128)S(1)} %bitcast.9), custom_call_target="tpu_custom_call" | custom-call | tf_op jit(solution)/shard_map/pallas_call | solution.py:652
  43.3 1.0 %copy.9 = f32[12,48,4,128]{3,2,1,0:T(4,128)} copy(f32[12,48,4,128]{3,2,1,0:T(4,128)S(1)} %bitcast.5) | data formatting | bytes 2359296
Async XLA Ops:
  0.0 1.3 %copy-start = (f32[12,48,4,128]{3,2,1,0:T(4,128)S(1)}, f32[12,48,4,128]{3,2,1,0:T(4,128)}, u32[]{:S(2)}) copy-start(f32[12,48,4,128]{3,2,1,0:T(4,128)} %param.7) | copy-start | bytes 3538948
  1.3 1.0 %copy-start.1 = (f32[12,48,128]{2,1,0:T(8,128)S(1)}, f32[12,48,128]{2,1,0:T(8,128)}, u32[]{:S(2)}) copy-start(f32[12,48,128]{2,1,0:T(8,128)} %param.8) | copy-start | bytes 884740
  2.2 0.7 %copy-start.2 = (f32[12,48]{1,0:T(8,128)S(1)}, f32[12,48]{1,0:T(8,128)}, u32[]{:S(2)}) copy-start(f32[12,48]{1,0:T(8,128)} %norm_ref.1) | copy-start | bytes 6916
  2.9 0.7 %copy-start.3 = (f32[12,48]{1,0:T(8,128)S(1)}, f32[12,48]{1,0:T(8,128)}, u32[]{:S(2)}) copy-start(f32[12,48]{1,0:T(8,128)} %lon_ref.1) | copy-start | bytes 6916
  3.6 0.7 %copy-start.4 = (f32[12,48]{1,0:T(8,128)S(1)}, f32[12,48]{1,0:T(8,128)}, u32[]{:S(2)}) copy-start(f32[12,48]{1,0:T(8,128)} %lat_ref.1) | copy-start | bytes 6916
  4.3 0.7 %copy-start.5 = (f32[128]{0:T(128)S(1)}, f32[128]{0:T(128)}, u32[]{:S(2)}) copy-start(f32[128]{0:T(128)} %param.12) | copy-start | bytes 1540
  5.0 0.7 %copy-start.6 = (f32[127]{0:T(128)S(1)}, f32[127]{0:T(128)}, u32[]{:S(2)}) copy-start(f32[127]{0:T(128)} %param.13) | copy-start | bytes 1528

commit v2 on v1

--- a/solution.py
+++ b/solution.py
@@ -22,8 +22,11 @@
 HALF = SHARE * SUB
 
 
-def solver_of(row, core):
-    return ((2 * row + core) * 4) // 3
+def lat_partner(band, step):
+    hop = step // 2
+    away = (2 + hop + hop // 2 + 2 * (hop // 3)) % (BANDS // 2)
+    other = (step + hop // 3) % 2
+    return (band // 2 + away) % (BANDS // 2) * 2 + (band + other) % 2
 
 
 def rows_at(start, count=SUB):
@@ -67,8 +70,8 @@
 
 
 def kernel(
-    e_hbm, g_hbm, norm_ref, lon_ref, lat_ref, diag_ref, below_ref, out_hbm,
-    e_v, g_v, out_v, y_v,
+    e_hbm, g_hbm, norm_hbm, lon_hbm, lat_hbm, diag_hbm, below_hbm, out_hbm,
+    e_v, g_v, norm_ref, lon_ref, lat_ref, diag_ref, below_ref, out_v, y_v,
     tmp, rk_t, phi_t, w1_t, n_t, phin_t, w1n_t,
     w1n_e, phin_e, w1_e, phi_e,
     lat_pad, lat_rk, lat_rows, lat_t, w1l_e, phil_e, cw1_e, cphi_e,
@@ -81,15 +84,14 @@
 ):
     band = lax.axis_index("lat")
     me = lax.axis_index("lon")
-    core = band % 2
-    place = me - me // 4
-    is_solver = jnp.logical_and(me % 4 != 3, place % 2 == core)
-    my_row = place // 2
-
-    loads = [
-        pltpu.make_async_copy(g_hbm, g_v, load_sem.at[0]),
-        pltpu.make_async_copy(e_hbm, e_v, load_sem.at[1]),
-    ]
+    is_solver = me < ROWS
+    my_row = me % ROWS
+
+    pairs = (
+        (lon_hbm, lon_ref), (norm_hbm, norm_ref), (lat_hbm, lat_ref), (g_hbm, g_v), (e_hbm, e_v),
+        (diag_hbm, diag_ref), (below_hbm, below_ref),
+    )
+    loads = [pltpu.make_async_copy(*pair, load_sem.at[k]) for k, pair in enumerate(pairs)]
     for copy in loads:
         copy.start()
 
@@ -103,10 +105,15 @@
         pl.semaphore_signal(barrier, inc=1, device_id=((band + step) % BANDS, me), device_id_type=MESH)
         return 0
 
-    lax.fori_loop(1, BLOCKS, greet_lon, 0)
+    @pl.when(is_solver)
+    def _():
+        lax.fori_loop(1, BLOCKS, greet_lon, 0)
+
     lax.fori_loop(1, BANDS, greet_lat, 0)
 
     tmp[...] = jnp.full((LEV, LEV), 2048.0, F32)
+    loads[0].wait()
+    loads[1].wait()
     tmp[0:ROWS, 0:COLS] = lon_ref[...]
     rk_t[...] = 1.0 / tmp[...].T[0:COLS]
     tmp[0:ROWS, 0:COLS] = norm_ref[...]
@@ -137,7 +144,13 @@
     w1n_t[...] = w1_t[...] * n_t[...]
     phin_t[...] = phi_t[...] * n_t[...]
 
-    pl.semaphore_wait(barrier, BLOCKS + BANDS - 2)
+    @pl.when(is_solver)
+    def _():
+        pl.semaphore_wait(barrier, ROWS + BANDS - 2)
+
+    @pl.when(jnp.logical_not(is_solver))
+    def _():
+        pl.semaphore_wait(barrier, ROWS + BANDS - 1)
 
     def coeff_copy_a(row):
         return pltpu.make_async_remote_copy(
@@ -145,7 +158,7 @@
             dst_ref=cr_a.at[rows_at(me * SUB)],
             send_sem=ca_send.at[row],
             recv_sem=ca_recv,
-            device_id=(band, solver_of(row, core)),
+            device_id=(band, row),
             device_id_type=MESH,
         )
 
@@ -155,7 +168,7 @@
             dst_ref=sr_a.at[rows_at(me * SUB)],
             send_sem=sa_send.at[row],
             recv_sem=sa_recv,
-            device_id=(band, solver_of(row, core)),
+            device_id=(band, row),
             device_id_type=MESH,
         )
 
@@ -191,7 +204,7 @@
     def send_coeff_a(step, _):
         row = (me + step) % ROWS
 
-        @pl.when(solver_of(row, core) != me)
+        @pl.when(row != me)
         def _():
             coeff_copy_a(row).start()
 
@@ -204,6 +217,7 @@
         cr_a[rows_at(me * SUB)] = cs_a[...]
 
     lat_pad[...] = jnp.full((16, LEV), 512.0, F32)
+    loads[2].wait()
     lat_pad[0:ROWS, 0:COLS] = lat_ref[...]
     lat_rk[...] = 1.0 / lat_pad[...]
     at = band * ROWS + lax.broadcasted_iota(jnp.int32, (16, LEV), 0)
@@ -259,8 +273,8 @@
                 at = j * COLS + t * SUB
                 target[at : at + SUB] = jnp.broadcast_to(part[:, j : j + 1], (SUB, LEV))
 
-    for copy in loads:
-        copy.wait()
+    loads[3].wait()
+    loads[4].wait()
 
     def contribute(step, _):
         row = (me + step) % ROWS
@@ -275,7 +289,7 @@
                 sums[MEMB + m] = sums[MEMB + m] + second * value
         ss_a[rows_at(row * SUB)] = sublane_sums(sums)
 
-        @pl.when(solver_of(row, core) != me)
+        @pl.when(row != me)
         def _():
             rhs_copy_a(row).start()
 
@@ -287,6 +301,8 @@
     def _():
         sr_a[rows_at(me * SUB)] = ss_a[rows_at(my_row * SUB)]
 
+    loads[5].wait()
+    loads[6].wait()
     tmp[0:SUB] = jnp.zeros((SUB, LEV), F32)
     tmp[0:1, 0 : LEV - 1] = below_ref[...]
     dinv = 1.0 / wide(diag_ref[...])
@@ -303,6 +319,100 @@
     vinv[...] = lax.dot_general(
         half, half, (((1,), (1,)), ((), ())), precision=HIGHEST, preferred_element_type=F32
     )
+
+    for t in range(RUN):
+        for source, target in ((w1_t, w1_e), (phi_t, phi_e)):
+            part = source[pl.ds(t, SUB, stride=RUN), :]
+            for j in range(ROWS):
+                at = j * COLS + t * SUB
+                target[at : at + SUB] = jnp.broadcast_to(part[:, j : j + 1], (SUB, LEV))
+
+    def interior(row, _):
+        firsts, seconds = [], []
+        for t in range(RUN):
+            grad = g_v[pl.ds(row * COLS + t, SUB, stride=RUN), :]
+            firsts.append(w1n_e[rows_at(row * COLS + t * SUB)] * grad)
+            seconds.append(phin_e[rows_at(row * COLS + t * SUB)] * grad)
+        for m in range(MEMB):
+            values = [
+                e_v[pl.ds(row * COLS * MEMB + t * MEMB + m, SUB, stride=RUN * MEMB), :] for t in range(RUN)
+            ]
+            ahead = [seconds[0] * values[0]]
+            for t in range(1, RUN):
+                ahead.append(ahead[-1] + seconds[t] * values[t])
+            behind = [None] * RUN
+            total = jnp.zeros((SUB, LEV), F32)
+            for t in reversed(range(RUN)):
+                behind[t] = total
+                total = total + firsts[t] * values[t]
+            before = sums_before(ahead[-1])
+            after = sums_after(total)
+            for t in range(RUN):
+                w1 = w1_e[rows_at(row * COLS + t * SUB)]
+                phi = phi_e[rows_at(row * COLS + t * SUB)]
+                y_v[rows_at(((m * RUN + t) * ROWS + row) * SUB)] = w1 * (before + ahead[t]) + phi * (
+                    after + behind[t]
+                )
+        return 0
+
+    lax.fori_loop(0, ROWS, interior, 0)
+
+    size = UNITS * SUB
+
+    def vertical(part, _):
+        at = rows_at(part * size, size)
+        y_v[at] = jnp.dot(y_v[at], vinv[...], precision=HIGHEST, preferred_element_type=F32)
+        return 0
+
+    lax.fori_loop(0, ROWS, vertical, 0)
+
+    lat_t[...] = lat_rows[...].T
+    for t in range(RUN):
+        part = lat_t[pl.ds(t, SUB, stride=RUN), :]
+        for number, target in enumerate((w1l_e, phil_e, cw1_e, cphi_e)):
+            for j in range(ROWS):
+                at = j * COLS + t * SUB
+                lane_at = number * 16 + j
+                target[at : at + SUB] = jnp.broadcast_to(part[:, lane_at : lane_at + 1], (SUB, LEV))
+
+    def wait_coeff_b(step, _):
+        landed_b(0, (band + step) % BANDS).wait()
+        return 0
+
+    lax.fori_loop(1, BANDS, wait_coeff_b, 0)
+    flow_p = jnp.zeros((1, LEV), F32)
+    flow_s = jnp.zeros((1, LEV), F32)
+    val_p = jnp.ones((1, LEV), F32)
+    val_s = jnp.ones((1, LEV), F32)
+
+    def band_base(p):
+        own = cr_b[p * SUB + 1 : p * SUB + 2]
+        return own if p == 0 else own + cr_b[(p - 1) * SUB + 2 : (p - 1) * SUB + 3]
+
+    def band_link(p):
+        return cr_b[p * SUB : p * SUB + 1]
+
+    rows_b[...] = jnp.zeros((LEV, LEV), F32)
+    rows_b[0:1] = val_p
+    rows_b[2 * BANDS - 1 : 2 * BANDS] = val_s
+    for p in range(BANDS - 1):
+        flow_p = flow_p + band_base(p) * val_p
+        val_p = val_p + flow_p / band_link(p)
+        rows_b[p + 1 : p + 2] = val_p
+        k = BANDS - 1 - p
+        flow_s = flow_s + band_base(k) * val_s
+        val_s = val_s + flow_s / band_link(k - 1)
+        rows_b[BANDS + k - 1 : BANDS + k] = val_s
+    flow_s = flow_s + band_base(0) * val_s
+    rows_b[BANDS : 2 * BANDS] = rows_b[BANDS : 2 * BANDS] * (1.0 / flow_s)
+    for p in range(BANDS - 1):
+        rows_b[2 * BANDS + p : 2 * BANDS + p + 1] = band_link(p)
+    tb_b[...] = rows_b[...].T
+    for tt in range(SHARE):
+        part = tb_b[pl.ds((band % 2) * SHARE + tt, SUB, stride=RUN), :]
+        for number in range(3 * BANDS):
+            at = (number * SHARE + tt) * SUB
+            el_b[at : at + SUB] = jnp.broadcast_to(part[:, number : number + 1], (SUB, LEV))
 
     @pl.when(is_solver)
     def _():
@@ -371,109 +481,18 @@
             ts_a[pl.ds(m, BLOCKS, stride=SUB), :] = found
             ts_a[pl.ds(MEMB + m, BLOCKS, stride=SUB), :] = link * pltpu.roll(found, BLOCKS - 1, 0)
 
-        def send_back(step, _):
-            back_copy_a((me + step) % BLOCKS).start()
+        def send_back(target, _):
+            @pl.when(target != me)
+            def _():
+                back_copy_a(target).start()
+
             return 0
 
-        lax.fori_loop(1, BLOCKS, send_back, 0)
+        lax.fori_loop(0, BLOCKS, send_back, 0)
         tr_a[rows_at(my_row * SUB)] = ts_a[rows_at(me * SUB)]
 
-    for t in range(RUN):
-        for source, target in ((w1_t, w1_e), (phi_t, phi_e)):
-            part = source[pl.ds(t, SUB, stride=RUN), :]
-            for j in range(ROWS):
-                at = j * COLS + t * SUB
-                target[at : at + SUB] = jnp.broadcast_to(part[:, j : j + 1], (SUB, LEV))
-
-    def interior(row, _):
-        firsts, seconds = [], []
-        for t in range(RUN):
-            grad = g_v[pl.ds(row * COLS + t, SUB, stride=RUN), :]
-            firsts.append(w1n_e[rows_at(row * COLS + t * SUB)] * grad)
-            seconds.append(phin_e[rows_at(row * COLS + t * SUB)] * grad)
-        for m in range(MEMB):
-            values = [
-                e_v[pl.ds(row * COLS * MEMB + t * MEMB + m, SUB, stride=RUN * MEMB), :] for t in range(RUN)
-            ]
-            ahead = [seconds[0] * values[0]]
-            for t in range(1, RUN):
-                ahead.append(ahead[-1] + seconds[t] * values[t])
-            behind = [None] * RUN
-            total = jnp.zeros((SUB, LEV), F32)
-            for t in reversed(range(RUN)):
-                behind[t] = total
-                total = total + firsts[t] * values[t]
-            before = sums_before(ahead[-1])
-            after = sums_after(total)
-            for t in range(RUN):
-                w1 = w1_e[rows_at(row * COLS + t * SUB)]
-                phi = phi_e[rows_at(row * COLS + t * SUB)]
-                y_v[rows_at(((m * RUN + t) * ROWS + row) * SUB)] = w1 * (before + ahead[t]) + phi * (
-                    after + behind[t]
-                )
-        return 0
-
-    lax.fori_loop(0, ROWS, interior, 0)
-
-    size = UNITS * SUB
-
-    def vertical(part, _):
-        at = rows_at(part * size, size)
-        y_v[at] = jnp.dot(y_v[at], vinv[...], precision=HIGHEST, preferred_element_type=F32)
-        return 0
-
-    lax.fori_loop(0, ROWS, vertical, 0)
-
-    lat_t[...] = lat_rows[...].T
-    for t in range(RUN):
-        part = lat_t[pl.ds(t, SUB, stride=RUN), :]
-        for number, target in enumerate((w1l_e, phil_e, cw1_e, cphi_e)):
-            for j in range(ROWS):
-                at = j * COLS + t * SUB
-                lane_at = number * 16 + j
-                target[at : at + SUB] = jnp.broadcast_to(part[:, lane_at : lane_at + 1], (SUB, LEV))
-
-    def wait_coeff_b(step, _):
-        landed_b(0, (band + step) % BANDS).wait()
-        return 0
-
-    lax.fori_loop(1, BANDS, wait_coeff_b, 0)
-    flow_p = jnp.zeros((1, LEV), F32)
-    flow_s = jnp.zeros((1, LEV), F32)
-    val_p = jnp.ones((1, LEV), F32)
-    val_s = jnp.ones((1, LEV), F32)
-
-    def band_base(p):
-        own = cr_b[p * SUB + 1 : p * SUB + 2]
-        return own if p == 0 else own + cr_b[(p - 1) * SUB + 2 : (p - 1) * SUB + 3]
-
-    def band_link(p):
-        return cr_b[p * SUB : p * SUB + 1]
-
-    rows_b[...] = jnp.zeros((LEV, LEV), F32)
-    rows_b[0:1] = val_p
-    rows_b[2 * BANDS - 1 : 2 * BANDS] = val_s
-    for p in range(BANDS - 1):
-        flow_p = flow_p + band_base(p) * val_p
-        val_p = val_p + flow_p / band_link(p)
-        rows_b[p + 1 : p + 2] = val_p
-        k = BANDS - 1 - p
-        flow_s = flow_s + band_base(k) * val_s
-        val_s = val_s + flow_s / band_link(k - 1)
-        rows_b[BANDS + k - 1 : BANDS + k] = val_s
-    flow_s = flow_s + band_base(0) * val_s
-    rows_b[BANDS : 2 * BANDS] = rows_b[BANDS : 2 * BANDS] * (1.0 / flow_s)
-    for p in range(BANDS - 1):
-        rows_b[2 * BANDS + p : 2 * BANDS + p + 1] = band_link(p)
-    tb_b[...] = rows_b[...].T
-    for tt in range(SHARE):
-        part = tb_b[pl.ds((band % 2) * SHARE + tt, SUB, stride=RUN), :]
-        for number in range(3 * BANDS):
-            at = (number * SHARE + tt) * SUB
-            el_b[at : at + SUB] = jnp.broadcast_to(part[:, number : number + 1], (SUB, LEV))
-
     def wait_back_a(row, _):
-        @pl.when(solver_of(row, core) != me)
+        @pl.when(row != me)
         def _():
             slot = tr_a.at[rows_at(row * SUB)]
             pltpu.make_async_copy(slot, slot, ta_recv.at[row]).wait()
@@ -483,7 +502,7 @@
     lax.fori_loop(0, ROWS, wait_back_a, 0)
 
     def finish_lon(step, _):
-        share = (band + 1 + step) % BANDS
+        share = lat_partner(band, step)
         m = share // 2
         for tt in range(SHARE):
             t = (share % 2) * SHARE + tt
@@ -566,14 +585,14 @@
             total = total + spread(BANDS + p) * rhs[p]
 
     def send_back_b(step, _):
-        copy_b(2, (band + step) % BANDS).start()
-        return 0
-
-    lax.fori_loop(1, BANDS, send_back_b, 0)
+        copy_b(2, lat_partner(band, step)).start()
+        return 0
+
+    lax.fori_loop(0, BANDS - 1, send_back_b, 0)
     tr_b[rows_at(band * 2 * HALF, 2 * HALF)] = ts_b[rows_at(band * 2 * HALF, 2 * HALF)]
 
     def finish(step, _):
-        share = (band + step) % BANDS
+        share = lat_partner(band, BANDS - 1 - step)
 
         @pl.when(share != band)
         def _():
@@ -597,7 +616,7 @@
     result.start()
 
     def sent_a(row, _):
-        @pl.when(solver_of(row, core) != me)
+        @pl.when(row != me)
         def _():
             coeff_copy_a(row).wait_send()
             rhs_copy_a(row).wait_send()
@@ -627,7 +646,6 @@
     ensemble, grad_increment, normalization, lon_diffusion, lat_diffusion, vert_diag, vert_sub
 ):
     block = ROWS * COLS * MEMB
-    vmem = pl.BlockSpec(memory_space=pltpu.VMEM)
     anywhere = pl.BlockSpec(memory_space=pl.ANY)
 
     def buf(rows):
@@ -636,7 +654,8 @@
     coeffs = ROWS * COLS
     dma = pltpu.SemaphoreType.DMA
     scratch = [
-        buf(block), buf(coeffs), buf(block), buf(block),
+        buf(block), buf(coeffs), *[pltpu.VMEM((ROWS, COLS), F32)] * 3, buf(1), pltpu.VMEM((1, LEV - 1), F32),
+        buf(block), buf(block),
         buf(LEV), *[buf(COLS)] * 6,
         *[buf(coeffs)] * 4,
         buf(16), buf(16), buf(LEV), buf(LEV), *[buf(coeffs)] * 4,
@@ -645,18 +664,18 @@
         buf(2 * BLOCKS), buf(2 * BLOCKS),
         buf(SUB), buf(BANDS * SUB), *[buf(BANDS * 2 * HALF)] * 4,
         buf(LEV), buf(LEV), buf(3 * BANDS * HALF),
-        dma((2,)), dma,
+        dma((7,)), dma,
         dma((ROWS,)), dma, dma((ROWS,)), dma, dma((BLOCKS,)), dma((ROWS,)),
         *[dma((BANDS,))] * 6,
     ]
     out = pl.pallas_call(
         kernel,
         out_shape=jax.ShapeDtypeStruct((block, LEV), F32),
-        in_specs=[anywhere, anywhere, vmem, vmem, vmem, vmem, vmem],
+        in_specs=[anywhere] * 7,
         out_specs=anywhere,
         scratch_shapes=scratch,
         compiler_params=pltpu.CompilerParams(
-            collective_id=0, has_side_effects=True, vmem_limit_bytes=32 * 1024 * 1024
+            collective_id=0, has_side_effects=True, vmem_limit_bytes=60 * 1024 * 1024
         ),
     )(
         ensemble.reshape(block, LEV),

time: 44.6 us -> 38 us (0.85)
  local copies, waits for them, and re-layouts: 6.65 us -> 2.36 us
  Pallas kernels: 37.6 us -> 35.5 us
    unnamed x15 -> x1, local copies, waits for them, and re-layouts: 6.65 us -> 2.36 us
    pallas_call x1, Pallas kernels: 37.6 us -> 35.5 us  [shards(): pl.pallas_call(kernel, out_shape=jax.ShapeDtypeStruct((block, LEV), F32),...]
where the time goes in v2:
time: 38 us; the launch traced here: 37.9 us
  Pallas kernels  35.5 us (93%)
  local copies, waits for them, and re-layouts  2.36 us (6%)
    pallas_call x1, Pallas kernels, shards(): pl.pallas_call(kernel, out_shape=jax.ShapeDtypeStruct((block, LEV), F32),...  35.5 us
    unnamed x1, local copies, waits for them, and re-layouts  2.36 us

profile of v2, /device:TPU:1, one launch (start us, length us, event | category | flops | bytes accessed | tf_op | source)
XLA Modules:
  0.0 37.9 jit_solution(11659931727046238314)
XLA Ops:
  0.0 35.5 %shard_map.73 = f32[2304,128]{1,0:T(8,128)} custom-call(f32[2304,128]{1,0:T(8,128)} %bitcast.6, f32[576,128]{1,0:T(8,128)} %bitcast.7, f32[12,48]{1,0:T(8,128)} %norm_hbm.1, f32[12,48]{1,0:T(8,128)} %lon_hbm.1, f32[12,48]{1,0:T(8,128)} %lat_hbm.1, f32[1,128]{1,0:T(1,128)} %bitcast.8, f32[1,127]{1,0:T(1,128)} %bitcast.9), custom_call_target="tpu_custom_call" | custom-call | tf_op jit(solution)/shard_map/pallas_call | solution.py:671
  35.5 2.4 %copy.9 = f32[12,48,4,128]{3,2,1,0:T(4,128)} copy(f32[12,48,4,128]{3,2,1,0:T(4,128)} %bitcast.5) | data formatting | bytes 2359296

commit v3 on v2

--- a/solution.py
+++ b/solution.py
@@ -70,15 +70,15 @@
 
 
 def kernel(
-    e_hbm, g_hbm, norm_hbm, lon_hbm, lat_hbm, diag_hbm, below_hbm, out_hbm,
-    e_v, g_v, norm_ref, lon_ref, lat_ref, diag_ref, below_ref, out_v, y_v,
+    e_hbm, g_hbm, norm_hbm, lon_hbm, lat_hbm, diag_hbm, below_hbm, out_v,
+    e_v, g_v, norm_ref, lon_ref, lat_ref, diag_ref, below_ref, y_v,
     tmp, rk_t, phi_t, w1_t, n_t, phin_t, w1n_t,
     w1n_e, phin_e, w1_e, phi_e,
     lat_pad, lat_rk, lat_rows, lat_t, w1l_e, phil_e, cw1_e, cphi_e,
     vinv,
     cs_a, cr_a, ss_a, sr_a, ts_a, tr_a, rows_a, inv_a,
     cs_b, cr_b, ss_b, sr_b, ts_b, tr_b, rows_b, tb_b, el_b,
-    load_sem, store_sem,
+    load_sem,
     ca_send, ca_recv, sa_send, sa_recv, ta_send, ta_recv,
     cb_send, cb_recv, sb_send, sb_recv, tb_send, tb_recv,
 ):
@@ -591,6 +591,31 @@
     lax.fori_loop(0, BANDS - 1, send_back_b, 0)
     tr_b[rows_at(band * 2 * HALF, 2 * HALF)] = ts_b[rows_at(band * 2 * HALF, 2 * HALF)]
 
+    def sent_a(row, _):
+        @pl.when(row != me)
+        def _():
+            coeff_copy_a(row).wait_send()
+            rhs_copy_a(row).wait_send()
+
+        return 0
+
+    lax.fori_loop(0, ROWS, sent_a, 0)
+
+    @pl.when(is_solver)
+    def _():
+        def sent_back(step, _):
+            back_copy_a((me + step) % BLOCKS).wait_send()
+            return 0
+
+        lax.fori_loop(1, BLOCKS, sent_back, 0)
+
+    def sent_b(step, _):
+        for kind in range(3):
+            copy_b(kind, (band + step) % BANDS).wait_send()
+        return 0
+
+    lax.fori_loop(1, BANDS, sent_b, 0)
+
     def finish(step, _):
         share = lat_partner(band, BANDS - 1 - step)
 
@@ -612,34 +637,6 @@
         return 0
 
     lax.fori_loop(0, BANDS, finish, 0)
-    result = pltpu.make_async_copy(out_v, out_hbm, store_sem)
-    result.start()
-
-    def sent_a(row, _):
-        @pl.when(row != me)
-        def _():
-            coeff_copy_a(row).wait_send()
-            rhs_copy_a(row).wait_send()
-
-        return 0
-
-    lax.fori_loop(0, ROWS, sent_a, 0)
-
-    @pl.when(is_solver)
-    def _():
-        def sent_back(step, _):
-            back_copy_a((me + step) % BLOCKS).wait_send()
-            return 0
-
-        lax.fori_loop(1, BLOCKS, sent_back, 0)
-
-    def sent_b(step, _):
-        for kind in range(3):
-            copy_b(kind, (band + step) % BANDS).wait_send()
-        return 0
-
-    lax.fori_loop(1, BANDS, sent_b, 0)
-    result.wait()
 
 
 def shards(
@@ -655,7 +652,7 @@
     dma = pltpu.SemaphoreType.DMA
     scratch = [
         buf(block), buf(coeffs), *[pltpu.VMEM((ROWS, COLS), F32)] * 3, buf(1), pltpu.VMEM((1, LEV - 1), F32),
-        buf(block), buf(block),
+        buf(block),
         buf(LEV), *[buf(COLS)] * 6,
         *[buf(coeffs)] * 4,
         buf(16), buf(16), buf(LEV), buf(LEV), *[buf(coeffs)] * 4,
@@ -664,15 +661,15 @@
         buf(2 * BLOCKS), buf(2 * BLOCKS),
         buf(SUB), buf(BANDS * SUB), *[buf(BANDS * 2 * HALF)] * 4,
         buf(LEV), buf(LEV), buf(3 * BANDS * HALF),
-        dma((7,)), dma,
+        dma((7,)),
         dma((ROWS,)), dma, dma((ROWS,)), dma, dma((BLOCKS,)), dma((ROWS,)),
         *[dma((BANDS,))] * 6,
     ]
     out = pl.pallas_call(
         kernel,
-        out_shape=jax.ShapeDtypeStruct((block, LEV), F32),
+        out_shape=pltpu.VMEM((block, LEV), F32),
         in_specs=[anywhere] * 7,
-        out_specs=anywhere,
+        out_specs=pl.BlockSpec(memory_space=pltpu.VMEM),
         scratch_shapes=scratch,
         compiler_params=pltpu.CompilerParams(
             collective_id=0, has_side_effects=True, vmem_limit_bytes=60 * 1024 * 1024

time: 38 us -> 35.6 us (0.937)
  local copies, waits for them, and re-layouts: 2.36 us -> 1.02 us
  Pallas kernels: 35.5 us -> 34.5 us
    unnamed x1, local copies, waits for them, and re-layouts: 2.36 us -> 1.02 us
    pallas_call x1, Pallas kernels: 35.5 us -> 34.5 us  [shards(): pl.pallas_call(kernel, out_shape=pltpu.VMEM((block, LEV), F32), in_specs=...]
where the time goes in v3:
time: 35.6 us; the launch traced here: 35.5 us
  Pallas kernels  34.5 us (97%)
  local copies, waits for them, and re-layouts  1.02 us (3%)
    pallas_call x1, Pallas kernels, shards(): pl.pallas_call(kernel, out_shape=pltpu.VMEM((block, LEV), F32), in_specs=...  34.5 us
    unnamed x1, local copies, waits for them, and re-layouts  1.02 us

profile of v3, /device:TPU:1, one launch (start us, length us, event | category | flops | bytes accessed | tf_op | source)
XLA Modules:
  0.0 35.5 jit_solution(10906612529713727840)
XLA Ops:
  0.0 34.5 %shard_map.73 = f32[2304,128]{1,0:T(8,128)S(1)} custom-call(f32[2304,128]{1,0:T(8,128)} %bitcast.6, f32[576,128]{1,0:T(8,128)} %bitcast.7, f32[12,48]{1,0:T(8,128)} %norm_hbm.1, f32[12,48]{1,0:T(8,128)} %lon_hbm.1, f32[12,48]{1,0:T(8,128)} %lat_hbm.1, f32[1,128]{1,0:T(1,128)} %bitcast.8, f32[1,127]{1,0:T(1,128)} %bitcast.9), custom_call_target="tpu_custom_call" | custom-call | tf_op jit(solution)/shard_map/pallas_call | solution.py:668
  34.5 1.0 %copy.9 = f32[12,48,4,128]{3,2,1,0:T(4,128)} copy(f32[12,48,4,128]{3,2,1,0:T(4,128)S(1)} %bitcast.5) | data formatting | bytes 2359296

commit v4 on v3

--- a/solution.py
+++ b/solution.py
@@ -35,6 +35,15 @@
 
 def wide(row, rows=SUB):
     return jnp.broadcast_to(row, (rows, LEV))
+
+
+def parts_of(value):
+    high = value.astype(jnp.bfloat16)
+    return high, (value - high.astype(F32)).astype(jnp.bfloat16)
+
+
+def product(left, right):
+    return jnp.dot(left, right, preferred_element_type=F32)
 
 
 def sublane_sums(vals):
@@ -136,10 +145,10 @@
         w1_t[k - 1 : k] = val_s
     edge = 1.0 / val_p
     scale = 1.0 / val_s
-    cs_a[...] = jnp.zeros((SUB, LEV), F32)
-    cs_a[0:1] = edge
-    cs_a[1:2] = 1.0 + flow_s * scale
-    cs_a[2:3] = flow_p * edge
+    lane = lax.broadcasted_iota(jnp.int32, (SUB, LEV), 1)
+    own = pltpu.roll(wide(1.0 + flow_s * scale), 16, 1)
+    after = pltpu.roll(wide(flow_p * edge), 32, 1)
+    cs_a[...] = jnp.where(lane < 16, wide(edge), jnp.where(lane < 32, own, after))
     w1_t[...] = w1_t[...] * scale
     w1n_t[...] = w1_t[...] * n_t[...]
     phin_t[...] = phi_t[...] * n_t[...]
@@ -154,8 +163,8 @@
 
     def coeff_copy_a(row):
         return pltpu.make_async_remote_copy(
-            src_ref=cs_a,
-            dst_ref=cr_a.at[rows_at(me * SUB)],
+            src_ref=cs_a.at[pl.ds(0, 1)],
+            dst_ref=cr_a.at[pl.ds(me, 1)],
             send_sem=ca_send.at[row],
             recv_sem=ca_recv,
             device_id=(band, row),
@@ -214,7 +223,7 @@
 
     @pl.when(is_solver)
     def _():
-        cr_a[rows_at(me * SUB)] = cs_a[...]
+        cr_a[pl.ds(me, 1)] = cs_a[0:1]
 
     lat_pad[...] = jnp.full((16, LEV), 512.0, F32)
     loads[2].wait()
@@ -416,10 +425,10 @@
 
     @pl.when(is_solver)
     def _():
-        slots = cr_a.at[rows_at(0, (BLOCKS - 1) * SUB)]
+        slots = cr_a.at[pl.ds(0, BLOCKS - 1)]
         pltpu.make_async_copy(slots, slots, ca_recv).wait()
-        link = cr_a[pl.ds(0, BLOCKS, stride=SUB), :]
-        base = cr_a[pl.ds(1, BLOCKS, stride=SUB), :] + pltpu.roll(cr_a[pl.ds(2, BLOCKS, stride=SUB), :], 1, 0)
+        link = cr_a[...]
+        base = pltpu.roll(link, LEV - 16, 1) + pltpu.roll(pltpu.roll(link, LEV - 32, 1), 1, 0)
         rows_a[0:BLOCKS] = 1.0 / link
         rows_a[BLOCKS : 2 * BLOCKS] = base
         flow_p = jnp.zeros((1, LEV), F32)
@@ -471,13 +480,21 @@
         slots = sr_a.at[rows_at(0, (BLOCKS - 1) * SUB)]
         pltpu.make_async_copy(slots, slots, sa_recv).wait()
         link = inv_a[BLOCKS : 2 * BLOCKS]
-        inverse = inv_a[0:BLOCKS][:, 0:BLOCKS]
+        inv_high, inv_low = parts_of(inv_a[0:BLOCKS][:, 0:BLOCKS])
+        vinv_high, vinv_low = parts_of(vinv[...])
+        rhs = []
         for m in range(MEMB):
             own = sr_a[pl.ds(m, BLOCKS, stride=SUB), :]
             after = sr_a[pl.ds(MEMB + m, BLOCKS, stride=SUB), :]
-            rhs = own + pltpu.roll(link * after, 1, 0)
-            rhs = jnp.dot(rhs, vinv[...], precision=HIGHEST, preferred_element_type=F32)
-            found = jnp.dot(inverse, rhs, precision=HIGHEST, preferred_element_type=F32)
+            rhs.append(own + pltpu.roll(link * after, 1, 0))
+        high, low = parts_of(jnp.concatenate(rhs, axis=0))
+        rhs = product(high, vinv_high) + product(high, vinv_low) + product(low, vinv_high)
+        high, low = parts_of(
+            jnp.concatenate([rhs[m * BLOCKS : (m + 1) * BLOCKS] for m in range(MEMB)], axis=1)
+        )
+        solved = product(inv_high, high) + product(inv_high, low) + product(inv_low, high)
+        for m in range(MEMB):
+            found = solved[:, m * LEV : (m + 1) * LEV]
             ts_a[pl.ds(m, BLOCKS, stride=SUB), :] = found
             ts_a[pl.ds(MEMB + m, BLOCKS, stride=SUB), :] = link * pltpu.roll(found, BLOCKS - 1, 0)
 
@@ -657,7 +674,7 @@
         *[buf(coeffs)] * 4,
         buf(16), buf(16), buf(LEV), buf(LEV), *[buf(coeffs)] * 4,
         buf(LEV),
-        buf(SUB), buf(BLOCKS * SUB), buf(ROWS * SUB), buf(BLOCKS * SUB), buf(BLOCKS * SUB), buf(ROWS * SUB),
+        buf(SUB), buf(BLOCKS), buf(ROWS * SUB), buf(BLOCKS * SUB), buf(BLOCKS * SUB), buf(ROWS * SUB),
         buf(2 * BLOCKS), buf(2 * BLOCKS),
         buf(SUB), buf(BANDS * SUB), *[buf(BANDS * 2 * HALF)] * 4,
         buf(LEV), buf(LEV), buf(3 * BANDS * HALF),

time: 35.6 us -> 32.8 us (0.921)
  Pallas kernels: 34.5 us -> 31.6 us
    pallas_call x1, Pallas kernels: 34.5 us -> 31.6 us  [shards(): pl.pallas_call(kernel, out_shape=pltpu.VMEM((block, LEV), F32), in_specs=...]
where the time goes in v4:
time: 32.8 us; the launch traced here: 32.7 us
  Pallas kernels  31.6 us (96%)
  local copies, waits for them, and re-layouts  1.02 us (3%)
    pallas_call x1, Pallas kernels, shards(): pl.pallas_call(kernel, out_shape=pltpu.VMEM((block, LEV), F32), in_specs=...  31.6 us
    unnamed x1, local copies, waits for them, and re-layouts  1.02 us

profile of v4, /device:TPU:1, one launch (start us, length us, event | category | flops | bytes accessed | tf_op | source)
XLA Modules:
  0.0 32.7 jit_solution(15771954868695501837)
XLA Ops:
  0.0 31.6 %shard_map.73 = f32[2304,128]{1,0:T(8,128)S(1)} custom-call(f32[2304,128]{1,0:T(8,128)} %bitcast.6, f32[576,128]{1,0:T(8,128)} %bitcast.7, f32[12,48]{1,0:T(8,128)} %norm_hbm.1, f32[12,48]{1,0:T(8,128)} %lon_hbm.1, f32[12,48]{1,0:T(8,128)} %lat_hbm.1, f32[1,128]{1,0:T(1,128)} %bitcast.8, f32[1,127]{1,0:T(1,128)} %bitcast.9), custom_call_target="tpu_custom_call" | custom-call | tf_op jit(solution)/shard_map/pallas_call | solution.py:685
  31.7 1.0 %copy.9 = f32[12,48,4,128]{3,2,1,0:T(4,128)} copy(f32[12,48,4,128]{3,2,1,0:T(4,128)S(1)} %bitcast.5) | data formatting | bytes 2359296

commit v5 on v4

--- a/solution.py
+++ b/solution.py
@@ -20,6 +20,10 @@
 SHARE = UNITS // BANDS
 NLAT = ROWS * BANDS
 HALF = SHARE * SUB
+SOLVERS = 6
+GROUP = ROWS // SOLVERS
+PACK = GROUP * SUB
+FIRST = 4
 
 
 def lat_partner(band, step):
@@ -93,8 +97,24 @@
 ):
     band = lax.axis_index("lat")
     me = lax.axis_index("lon")
-    is_solver = me < ROWS
-    my_row = me % ROWS
+    is_solver = jnp.logical_and(me >= FIRST, me < FIRST + SOLVERS)
+    place = (me + SOLVERS - FIRST) % SOLVERS
+    seat = (me + BLOCKS - FIRST) % BLOCKS
+
+    barrier = pltpu.get_barrier_semaphore()
+
+    def greet_lon(step, _):
+        away = BLOCKS // 2 + (step + 1) // 2 * (1 - step % 2 * 2)
+        pl.semaphore_signal(barrier, inc=1, device_id=(band, (me + away) % BLOCKS), device_id_type=MESH)
+        return 0
+
+    def greet_lat(step, _):
+        pl.semaphore_signal(barrier, inc=1, device_id=((band + step) % BANDS, me), device_id_type=MESH)
+        return 0
+
+    @pl.when(is_solver)
+    def _():
+        lax.fori_loop(0, BLOCKS - 1, greet_lon, 0)
 
     pairs = (
         (lon_hbm, lon_ref), (norm_hbm, norm_ref), (lat_hbm, lat_ref), (g_hbm, g_v), (e_hbm, e_v),
@@ -103,20 +123,6 @@
     loads = [pltpu.make_async_copy(*pair, load_sem.at[k]) for k, pair in enumerate(pairs)]
     for copy in loads:
         copy.start()
-
-    barrier = pltpu.get_barrier_semaphore()
-
-    def greet_lon(step, _):
-        pl.semaphore_signal(barrier, inc=1, device_id=(band, (me + step) % BLOCKS), device_id_type=MESH)
-        return 0
-
-    def greet_lat(step, _):
-        pl.semaphore_signal(barrier, inc=1, device_id=((band + step) % BANDS, me), device_id_type=MESH)
-        return 0
-
-    @pl.when(is_solver)
-    def _():
-        lax.fori_loop(1, BLOCKS, greet_lon, 0)
 
     lax.fori_loop(1, BANDS, greet_lat, 0)
 
@@ -155,38 +161,38 @@
 
     @pl.when(is_solver)
     def _():
-        pl.semaphore_wait(barrier, ROWS + BANDS - 2)
+        pl.semaphore_wait(barrier, SOLVERS + BANDS - 2)
 
     @pl.when(jnp.logical_not(is_solver))
     def _():
-        pl.semaphore_wait(barrier, ROWS + BANDS - 1)
-
-    def coeff_copy_a(row):
+        pl.semaphore_wait(barrier, SOLVERS + BANDS - 1)
+
+    def coeff_copy_a(solver):
         return pltpu.make_async_remote_copy(
             src_ref=cs_a.at[pl.ds(0, 1)],
             dst_ref=cr_a.at[pl.ds(me, 1)],
-            send_sem=ca_send.at[row],
+            send_sem=ca_send.at[solver],
             recv_sem=ca_recv,
-            device_id=(band, row),
+            device_id=(band, solver + FIRST),
             device_id_type=MESH,
         )
 
-    def rhs_copy_a(row):
+    def rhs_copy_a(solver):
         return pltpu.make_async_remote_copy(
-            src_ref=ss_a.at[rows_at(row * SUB)],
-            dst_ref=sr_a.at[rows_at(me * SUB)],
-            send_sem=sa_send.at[row],
+            src_ref=ss_a.at[rows_at(solver * PACK, PACK)],
+            dst_ref=sr_a.at[rows_at(me * PACK, PACK)],
+            send_sem=sa_send.at[solver],
             recv_sem=sa_recv,
-            device_id=(band, row),
+            device_id=(band, solver + FIRST),
             device_id_type=MESH,
         )
 
     def back_copy_a(target):
         return pltpu.make_async_remote_copy(
-            src_ref=ts_a.at[rows_at(target * SUB)],
-            dst_ref=tr_a.at[rows_at(my_row * SUB)],
+            src_ref=ts_a.at[rows_at(target * PACK, PACK)],
+            dst_ref=tr_a.at[rows_at(place * PACK, PACK)],
             send_sem=ta_send.at[target],
-            recv_sem=ta_recv.at[my_row],
+            recv_sem=ta_recv.at[place],
             device_id=(band, target),
             device_id_type=MESH,
         )
@@ -211,19 +217,56 @@
         return pltpu.make_async_copy(slot, slot, (cb_recv, sb_recv, tb_recv)[kind].at[source])
 
     def send_coeff_a(step, _):
-        row = (me + step) % ROWS
-
-        @pl.when(row != me)
+        solver = (me + step) % SOLVERS
+
+        @pl.when(solver != seat)
         def _():
-            coeff_copy_a(row).start()
-
-        return 0
-
-    lax.fori_loop(0, ROWS, send_coeff_a, 0)
+            coeff_copy_a(solver).start()
+
+        return 0
+
+    lax.fori_loop(0, SOLVERS, send_coeff_a, 0)
 
     @pl.when(is_solver)
     def _():
         cr_a[pl.ds(me, 1)] = cs_a[0:1]
+
+    for t in range(RUN):
+        for source, target in ((w1n_t, w1n_e), (phin_t, phin_e)):
+            part = source[pl.ds(t, SUB, stride=RUN), :]
+            for j in range(ROWS):
+                at = j * COLS + t * SUB
+                target[at : at + SUB] = jnp.broadcast_to(part[:, j : j + 1], (SUB, LEV))
+
+    loads[3].wait()
+    loads[4].wait()
+
+    def contribute(step, _):
+        solver = (me + step) % SOLVERS
+        for g in range(GROUP):
+            row = solver * GROUP + g
+            sums = [jnp.zeros((SUB, LEV), F32) for _ in range(2 * MEMB)]
+            for t in range(RUN):
+                grad = g_v[pl.ds(row * COLS + t, SUB, stride=RUN), :]
+                first = w1n_e[rows_at(row * COLS + t * SUB)] * grad
+                second = phin_e[rows_at(row * COLS + t * SUB)] * grad
+                for m in range(MEMB):
+                    value = e_v[pl.ds(row * COLS * MEMB + t * MEMB + m, SUB, stride=RUN * MEMB), :]
+                    sums[m] = sums[m] + first * value
+                    sums[MEMB + m] = sums[MEMB + m] + second * value
+            ss_a[rows_at(row * SUB)] = sublane_sums(sums)
+
+        @pl.when(solver != seat)
+        def _():
+            rhs_copy_a(solver).start()
+
+        return 0
+
+    lax.fori_loop(0, SOLVERS, contribute, 0)
+
+    @pl.when(is_solver)
+    def _():
+        sr_a[rows_at(me * PACK, PACK)] = ss_a[rows_at(place * PACK, PACK)]
 
     lat_pad[...] = jnp.full((16, LEV), 512.0, F32)
     loads[2].wait()
@@ -274,41 +317,6 @@
 
     lax.fori_loop(1, BANDS, send_coeff_b, 0)
     cr_b[rows_at(band * SUB)] = cs_b[...]
-
-    for t in range(RUN):
-        for source, target in ((w1n_t, w1n_e), (phin_t, phin_e)):
-            part = source[pl.ds(t, SUB, stride=RUN), :]
-            for j in range(ROWS):
-                at = j * COLS + t * SUB
-                target[at : at + SUB] = jnp.broadcast_to(part[:, j : j + 1], (SUB, LEV))
-
-    loads[3].wait()
-    loads[4].wait()
-
-    def contribute(step, _):
-        row = (me + step) % ROWS
-        sums = [jnp.zeros((SUB, LEV), F32) for _ in range(2 * MEMB)]
-        for t in range(RUN):
-            grad = g_v[pl.ds(row * COLS + t, SUB, stride=RUN), :]
-            first = w1n_e[rows_at(row * COLS + t * SUB)] * grad
-            second = phin_e[rows_at(row * COLS + t * SUB)] * grad
-            for m in range(MEMB):
-                value = e_v[pl.ds(row * COLS * MEMB + t * MEMB + m, SUB, stride=RUN * MEMB), :]
-                sums[m] = sums[m] + first * value
-                sums[MEMB + m] = sums[MEMB + m] + second * value
-        ss_a[rows_at(row * SUB)] = sublane_sums(sums)
-
-        @pl.when(row != me)
-        def _():
-            rhs_copy_a(row).start()
-
-        return 0
-
-    lax.fori_loop(0, ROWS, contribute, 0)
-
-    @pl.when(is_solver)
-    def _():
-        sr_a[rows_at(me * SUB)] = ss_a[rows_at(my_row * SUB)]
 
     loads[5].wait()
     loads[6].wait()
@@ -455,48 +463,54 @@
         tmp[3 * BLOCKS : 4 * BLOCKS] = both
         whole = tmp[...]
         lanes = lax.broadcasted_iota(jnp.int32, (LEV, LEV), 1)
-        column = jnp.sum(jnp.where(lanes == my_row, whole, 0.0), axis=1, keepdims=True)
-        column = jnp.broadcast_to(column, (LEV, LEV))
+        columns = []
+        for g in range(GROUP):
+            column = jnp.sum(jnp.where(lanes == place * GROUP + g, whole, 0.0), axis=1, keepdims=True)
+            columns.append(jnp.broadcast_to(column, (LEV, LEV)))
         tmp[...] = whole.T
-        line = wide(tmp[pl.ds(my_row, 1), :])
-        phi_row = wide(line[0:1], BLOCKS)
-        first_row = wide(pltpu.roll(line, LEV - BLOCKS, 1)[0:1], BLOCKS)
-        both_row = wide(pltpu.roll(line, LEV - 2 * BLOCKS, 1)[0:1], BLOCKS)
         sub_ids = lax.broadcasted_iota(jnp.int32, (BLOCKS, LEV), 0)
         lane_ids = lax.broadcasted_iota(jnp.int32, (BLOCKS, LEV), 1)
-        inv_a[0:BLOCKS] = (
-            jnp.where(
-                sub_ids <= lane_ids,
-                column[0:BLOCKS] * first_row,
-                column[BLOCKS : 2 * BLOCKS] * phi_row,
+        for g, column in enumerate(columns):
+            line = wide(tmp[pl.ds(place * GROUP + g, 1), :])
+            phi_row = wide(line[0:1], BLOCKS)
+            first_row = wide(pltpu.roll(line, LEV - BLOCKS, 1)[0:1], BLOCKS)
+            both_row = wide(pltpu.roll(line, LEV - 2 * BLOCKS, 1)[0:1], BLOCKS)
+            at = 2 * g * BLOCKS
+            inv_a[at : at + BLOCKS] = (
+                jnp.where(
+                    sub_ids <= lane_ids,
+                    column[0:BLOCKS] * first_row,
+                    column[BLOCKS : 2 * BLOCKS] * phi_row,
+                )
+                + column[3 * BLOCKS : 4 * BLOCKS] * both_row
             )
-            + column[3 * BLOCKS : 4 * BLOCKS] * both_row
-        )
-        link = jnp.sum(jnp.where(lane_ids == my_row, link, 0.0), axis=1, keepdims=True)
-        inv_a[BLOCKS : 2 * BLOCKS] = jnp.broadcast_to(link, (BLOCKS, LEV))
+            edge = jnp.sum(jnp.where(lane_ids == place * GROUP + g, link, 0.0), axis=1, keepdims=True)
+            inv_a[at + BLOCKS : at + 2 * BLOCKS] = jnp.broadcast_to(edge, (BLOCKS, LEV))
 
     @pl.when(is_solver)
     def _():
-        slots = sr_a.at[rows_at(0, (BLOCKS - 1) * SUB)]
+        vinv_high, vinv_low = parts_of(vinv[...])
+        slots = sr_a.at[rows_at(0, (BLOCKS - 1) * PACK)]
         pltpu.make_async_copy(slots, slots, sa_recv).wait()
-        link = inv_a[BLOCKS : 2 * BLOCKS]
-        inv_high, inv_low = parts_of(inv_a[0:BLOCKS][:, 0:BLOCKS])
-        vinv_high, vinv_low = parts_of(vinv[...])
-        rhs = []
-        for m in range(MEMB):
-            own = sr_a[pl.ds(m, BLOCKS, stride=SUB), :]
-            after = sr_a[pl.ds(MEMB + m, BLOCKS, stride=SUB), :]
-            rhs.append(own + pltpu.roll(link * after, 1, 0))
-        high, low = parts_of(jnp.concatenate(rhs, axis=0))
-        rhs = product(high, vinv_high) + product(high, vinv_low) + product(low, vinv_high)
-        high, low = parts_of(
-            jnp.concatenate([rhs[m * BLOCKS : (m + 1) * BLOCKS] for m in range(MEMB)], axis=1)
-        )
-        solved = product(inv_high, high) + product(inv_high, low) + product(inv_low, high)
-        for m in range(MEMB):
-            found = solved[:, m * LEV : (m + 1) * LEV]
-            ts_a[pl.ds(m, BLOCKS, stride=SUB), :] = found
-            ts_a[pl.ds(MEMB + m, BLOCKS, stride=SUB), :] = link * pltpu.roll(found, BLOCKS - 1, 0)
+        for g in range(GROUP):
+            inverse = inv_a[2 * g * BLOCKS : (2 * g + 1) * BLOCKS]
+            link = inv_a[(2 * g + 1) * BLOCKS : (2 * g + 2) * BLOCKS]
+            inv_high, inv_low = parts_of(inverse[:, 0:BLOCKS])
+            rhs = []
+            for m in range(MEMB):
+                own = sr_a[pl.ds(g * SUB + m, BLOCKS, stride=PACK), :]
+                after = sr_a[pl.ds(g * SUB + MEMB + m, BLOCKS, stride=PACK), :]
+                rhs.append(own + pltpu.roll(link * after, 1, 0))
+            high, low = parts_of(jnp.concatenate(rhs, axis=0))
+            rhs = product(high, vinv_high) + product(high, vinv_low) + product(low, vinv_high)
+            high, low = parts_of(
+                jnp.concatenate([rhs[m * BLOCKS : (m + 1) * BLOCKS] for m in range(MEMB)], axis=1)
+            )
+            solved = product(inv_high, high) + product(inv_high, low) + product(inv_low, high)
+            for m in range(MEMB):
+                found = solved[:, m * LEV : (m + 1) * LEV]
+                ts_a[pl.ds(g * SUB + m, BLOCKS, stride=PACK), :] = found
+                ts_a[pl.ds(g * SUB + MEMB + m, BLOCKS, stride=PACK), :] = link * pltpu.roll(found, BLOCKS - 1, 0)
 
         def send_back(target, _):
             @pl.when(target != me)
@@ -506,17 +520,17 @@
             return 0
 
         lax.fori_loop(0, BLOCKS, send_back, 0)
-        tr_a[rows_at(my_row * SUB)] = ts_a[rows_at(me * SUB)]
-
-    def wait_back_a(row, _):
-        @pl.when(row != me)
+        tr_a[rows_at(place * PACK, PACK)] = ts_a[rows_at(me * PACK, PACK)]
+
+    def wait_back_a(solver, _):
+        @pl.when(solver != seat)
         def _():
-            slot = tr_a.at[rows_at(row * SUB)]
-            pltpu.make_async_copy(slot, slot, ta_recv.at[row]).wait()
-
-        return 0
-
-    lax.fori_loop(0, ROWS, wait_back_a, 0)
+            slot = tr_a.at[rows_at(solver * PACK, PACK)]
+            pltpu.make_async_copy(slot, slot, ta_recv.at[solver]).wait()
+
+        return 0
+
+    lax.fori_loop(0, SOLVERS, wait_back_a, 0)
 
     def finish_lon(step, _):
         share = lat_partner(band, step)
@@ -602,21 +616,26 @@
             total = total + spread(BANDS + p) * rhs[p]
 
     def send_back_b(step, _):
-        copy_b(2, lat_partner(band, step)).start()
-        return 0
-
-    lax.fori_loop(0, BANDS - 1, send_back_b, 0)
+        target = (2 * step + 1 - step // (BANDS // 2)) % BANDS
+
+        @pl.when(target != band)
+        def _():
+            copy_b(2, target).start()
+
+        return 0
+
+    lax.fori_loop(0, BANDS, send_back_b, 0)
     tr_b[rows_at(band * 2 * HALF, 2 * HALF)] = ts_b[rows_at(band * 2 * HALF, 2 * HALF)]
 
-    def sent_a(row, _):
-        @pl.when(row != me)
+    def sent_a(solver, _):
+        @pl.when(solver != seat)
         def _():
-            coeff_copy_a(row).wait_send()
-            rhs_copy_a(row).wait_send()
-
-        return 0
-
-    lax.fori_loop(0, ROWS, sent_a, 0)
+            coeff_copy_a(solver).wait_send()
+            rhs_copy_a(solver).wait_send()
+
+        return 0
+
+    lax.fori_loop(0, SOLVERS, sent_a, 0)
 
     @pl.when(is_solver)
     def _():
@@ -674,12 +693,12 @@
         *[buf(coeffs)] * 4,
         buf(16), buf(16), buf(LEV), buf(LEV), *[buf(coeffs)] * 4,
         buf(LEV),
-        buf(SUB), buf(BLOCKS), buf(ROWS * SUB), buf(BLOCKS * SUB), buf(BLOCKS * SUB), buf(ROWS * SUB),
-        buf(2 * BLOCKS), buf(2 * BLOCKS),
+        buf(SUB), buf(BLOCKS), buf(ROWS * SUB), buf(BLOCKS * PACK), buf(BLOCKS * PACK), buf(ROWS * SUB),
+        buf(2 * BLOCKS), buf(2 * GROUP * BLOCKS),
         buf(SUB), buf(BANDS * SUB), *[buf(BANDS * 2 * HALF)] * 4,
         buf(LEV), buf(LEV), buf(3 * BANDS * HALF),
         dma((7,)),
-        dma((ROWS,)), dma, dma((ROWS,)), dma, dma((BLOCKS,)), dma((ROWS,)),
+        dma((SOLVERS,)), dma, dma((SOLVERS,)), dma, dma((BLOCKS,)), dma((SOLVERS,)),
         *[dma((BANDS,))] * 6,
     ]
     out = pl.pallas_call(

time: 32.8 us -> 31.2 us (0.951)
  Pallas kernels: 31.6 us -> 30.1 us
    pallas_call x1, Pallas kernels: 31.6 us -> 30.1 us  [shards(): pl.pallas_call(kernel, out_shape=pltpu.VMEM((block, LEV), F32), in_specs=...]
where the time goes in v5:
time: 31.2 us; the launch traced here: 31.1 us
  Pallas kernels  30.1 us (96%)
  local copies, waits for them, and re-layouts  1.02 us (3%)
    pallas_call x1, Pallas kernels, shards(): pl.pallas_call(kernel, out_shape=pltpu.VMEM((block, LEV), F32), in_specs=...  30.1 us
    unnamed x1, local copies, waits for them, and re-layouts  1.02 us

profile of v5, /device:TPU:1, one launch (start us, length us, event | category | flops | bytes accessed | tf_op | source)
XLA Modules:
  0.0 31.1 jit_solution(13921262434516632990)
XLA Ops:
  0.0 30.1 %shard_map.73 = f32[2304,128]{1,0:T(8,128)S(1)} custom-call(f32[2304,128]{1,0:T(8,128)} %bitcast.6, f32[576,128]{1,0:T(8,128)} %bitcast.7, f32[12,48]{1,0:T(8,128)} %norm_hbm.1, f32[12,48]{1,0:T(8,128)} %lon_hbm.1, f32[12,48]{1,0:T(8,128)} %lat_hbm.1, f32[1,128]{1,0:T(1,128)} %bitcast.8, f32[1,127]{1,0:T(1,128)} %bitcast.9), custom_call_target="tpu_custom_call" | custom-call | tf_op jit(solution)/shard_map/pallas_call | solution.py:704
  30.1 1.0 %copy.9 = f32[12,48,4,128]{3,2,1,0:T(4,128)} copy(f32[12,48,4,128]{3,2,1,0:T(4,128)S(1)} %bitcast.5) | data formatting | bytes 2359296

commit v6 on v5

--- a/solution.py
+++ b/solution.py
@@ -262,7 +262,7 @@
 
         return 0
 
-    lax.fori_loop(0, SOLVERS, contribute, 0)
+    lax.fori_loop(0, SOLVERS, contribute, 0, unroll=2)
 
     @pl.when(is_solver)
     def _():

time: 31.2 us -> 31.2 us (level)
  no operation moved by 1% of the time
where the time goes in v6:
time: 31.2 us; the launch traced here: 31.1 us
  Pallas kernels  30.1 us (96%)
  local copies, waits for them, and re-layouts  1.02 us (3%)
    pallas_call x1, Pallas kernels, shards(): pl.pallas_call(kernel, out_shape=pltpu.VMEM((block, LEV), F32), in_specs=...  30.1 us
    unnamed x1, local copies, waits for them, and re-layouts  1.02 us

profile of v6, /device:TPU:1, one launch (start us, length us, event | category | flops | bytes accessed | tf_op | source)
XLA Modules:
  0.0 31.1 jit_solution(6341394321690739079)
XLA Ops:
  0.0 30.1 %shard_map.73 = f32[2304,128]{1,0:T(8,128)S(1)} custom-call(f32[2304,128]{1,0:T(8,128)} %bitcast.6, f32[576,128]{1,0:T(8,128)} %bitcast.7, f32[12,48]{1,0:T(8,128)} %norm_hbm.1, f32[12,48]{1,0:T(8,128)} %lon_hbm.1, f32[12,48]{1,0:T(8,128)} %lat_hbm.1, f32[1,128]{1,0:T(1,128)} %bitcast.8, f32[1,127]{1,0:T(1,128)} %bitcast.9), custom_call_target="tpu_custom_call" | custom-call | tf_op jit(solution)/shard_map/pallas_call | solution.py:704
  30.1 1.0 %copy.9 = f32[12,48,4,128]{3,2,1,0:T(4,128)} copy(f32[12,48,4,128]{3,2,1,0:T(4,128)S(1)} %bitcast.5) | data formatting | bytes 2359296
